TPU v7x, 32 devices: a whole 2x2x4 slice. The times are simulated.
32 devices in a mesh: clips: 2 (over y), frame: 4 (over x, core), row: 4 (over z).
Axes of the slice: x: 2, y: 2, z: 4, core: 2. Of those that a mesh axis runs over, the one named last changes fastest.
Arguments:
- frames: bfloat16 [16, 512, 640], P(('clips', 'frame'), 'row'), parts along dimension 0, may hold values from -16 to 16
- key_index: int32 [4], P('clips'), parts along dimension 0, may hold values from 0 to 7, as said below
- w_query: bfloat16 [640, 640], replicated, may hold values from -0.25 to 0.25
- w_keyval: bfloat16 [640, 1280], replicated, may hold values from -0.25 to 0.25
- w_out: bfloat16 [640, 640], replicated, may hold values from -0.25 to 0.25
- norm_gain: float32 [640], replicated, may hold values from 0.1 to 1.9
- w_first: bfloat16 [3, 640, 640], replicated, may hold values from -0.125 to 0.125
- w_second: bfloat16 [3, 640, 640], replicated, may hold values from -0.125 to 0.125
Outputs:
- edited: bfloat16 [16, 512, 640], P(('clips', 'frame'), 'row'), parts along dimension 0
There are 2 independent parts, one for each index of `clips`. A program takes and returns all parts, laid end to end along the dimension named above; an argument that names none is the same for every part. Nothing has to cross between parts.
Inputs may be any that keep to these rules, and one draw needn't show every extreme that they name: `key_index`: two different frame indices of the window, in either order; one of them is the window's last frame 8 - 1.
All inputs are finite; a program needn't handle non-finite values.
Results may differ from a plain program's by a relative error of at most 0.0067.
Values may be sent and summed in bfloat16 or wider, within the bound.
A program may use at most 128 MiB of HBM per device.

v0:
```python
from functools import partial

import jax
import jax.numpy as jnp
from jax import lax
from jax.sharding import PartitionSpec as P

HEADS = 10
HEAD_DIM = 64


def from_root(value, axis, source):
    kept = jnp.where(lax.axis_index(axis) == source, value, 0).astype(value.dtype)
    return lax.psum(kept, axis)


def extended(array, sides, width):
    for axis, dim in sides:
        size, length = (lax.axis_size(axis), array.shape[dim])
        up = [(i, (i + 1) % size) for i in range(size - 1)]
        down = [(j, i) for i, j in up]
        last = lax.slice_in_dim(array, length - width, length, axis=dim)
        first = lax.slice_in_dim(array, 0, width, axis=dim)
        before = lax.ppermute(last, axis, up)
        after = lax.ppermute(first, axis, down)
        array = jnp.concatenate([before, array, after], axis=dim)
    return array


def temporal_mix(padded, weights, count):
    result = jnp.zeros((count * padded.shape[1], padded.shape[2]), jnp.float32)
    for offset in range(3):
        window = padded[offset : offset + count].reshape(-1, padded.shape[2])
        result = result + jnp.dot(window, weights[offset], preferred_element_type=jnp.float32)
    return result


def absorb_keys(query_heads, channels, state_now, kv_pieces, piece_start):
    highest, denominator, accumulated = state_now
    joined = jnp.concatenate(kv_pieces, axis=0)
    key_heads = joined[:, :channels].reshape(-1, HEADS, HEAD_DIM)
    value_heads = joined[:, channels:].reshape(-1, HEADS, HEAD_DIM)
    scores = jnp.einsum(
        "qhd,khd->hqk", query_heads, key_heads, preferred_element_type=jnp.float32
    ) * HEAD_DIM ** (-0.5)
    raised = jnp.maximum(highest, jnp.max(scores, axis=-1))
    kept_frac = jnp.exp(highest - raised)
    exponent = jnp.exp(scores - raised[:, :, None])
    denominator = jnp.sum(exponent, axis=-1)
    contrib = jnp.einsum(
        "hqk,khd->qhd",
        exponent.astype(jnp.bfloat16),
        value_heads,
        preferred_element_type=jnp.float32,
    )
    accumulated = accumulated * jnp.repeat(kept_frac.T, HEAD_DIM, axis=1) + contrib.reshape(
        contrib.shape[0], -1
    )
    return (raised, denominator, accumulated)


def shards(frames, key_index, w_query, w_keyval, w_out, norm_gain, w_first, w_second):
    frame_count, row_count, channels = frames.shape
    flattened = frames.reshape(-1, channels)
    queries = jnp.dot(flattened, w_query, preferred_element_type=jnp.float32).astype(jnp.bfloat16)
    query_heads = queries.reshape(-1, HEADS, HEAD_DIM)
    query_total = queries.shape[0]
    owners = key_index // frame_count
    chosen = frames[key_index % frame_count].reshape(-1, channels)
    keyval = jnp.dot(chosen, w_keyval, preferred_element_type=jnp.float32).astype(jnp.bfloat16)
    own_parts = (keyval[:row_count], keyval[row_count:])
    initial = (
        jnp.full((HEADS, query_total), -1e30, jnp.float32),
        jnp.zeros((HEADS, query_total), jnp.float32),
        jnp.zeros((query_total, channels), jnp.float32),
    )
    absorb = partial(absorb_keys, query_heads, channels)
    spread_parts = []
    for key_slot in range(2):
        spread_parts.append(from_root(own_parts[key_slot], "frame", owners[key_slot]))
    final = absorb(
        initial,
        (
            lax.all_gather(spread_parts[0], "row", axis=0, tiled=True),
            lax.all_gather(spread_parts[1], "row", axis=0, tiled=True),
        ),
        jnp.int32(0),
    )
    highest, denominator, accumulated = final
    mixed = accumulated.reshape(query_total, HEADS, HEAD_DIM) / denominator.T[:, :, None]
    attended = mixed.reshape(query_total, channels).astype(jnp.bfloat16)
    residual = flattened.astype(jnp.float32) + jnp.dot(
        attended, w_out, preferred_element_type=jnp.float32
    )
    mean_square = jnp.mean(residual * residual, axis=-1, keepdims=True)
    normed = (residual * lax.rsqrt(mean_square + 1e-06) * norm_gain).astype(jnp.bfloat16)
    normed = normed.reshape(frame_count, row_count, channels)
    padded = extended(normed, (("frame", 0),), 1)
    hidden = jax.nn.silu(temporal_mix(padded, w_first, frame_count)).astype(jnp.bfloat16)
    hidden = hidden.reshape(frame_count, row_count, channels)
    padded = extended(hidden, (("frame", 0),), 1)
    second = temporal_mix(padded, w_second, frame_count)
    return (residual + second).astype(jnp.bfloat16).reshape(frame_count, row_count, channels)


def solution(mesh):
    return jax.shard_map(
        shards,
        mesh=mesh,
        in_specs=(P(("clips", "frame"), "row", None), P("clips"), P(), P(), P(), P(), P(), P()),
        out_specs=P(("clips", "frame"), "row", None),
        check_vma=False,
    )
```

profile of v0, /device:TPU:1, one launch (start us, length us, event | category | flops | bytes accessed | tf_op | source)
XLA Modules:
  0.0 162.4 jit_solution(13678371207064377667)
XLA Ops:
  6.5 0.8 and_select_fusion.1
  7.3 0.6 fusion.42
  9.2 1.6 gather_fusion
  10.8 0.7 convolution_convert_fusion
  11.5 0.9 slice_select_fusion
  12.5 34.7 %all-reduce.3.cloned.1.call-done = (bf16[128,1280]{1,0:T(8,128)(2,1)}, bf16[128,1280]{1,0:T(8,128)(2,1)}) async-done(((bf16[128,1280]{1,0:T(8,128)(2,1)}, bf16[128,1280]{1,0:T(8,128)(2,1)}), (bf16[128,1280]{1,0:T(8,128)(2,1)}, bf16[128,1280]{1,0:T(8,128)(2,1)})) %all-reduce.3.cloned.1.call-update) | async-done | bytes 655376 | tf_op jit(solution)/shard_map/psum | solution.py:14
  47.3 0.7 all-gather.5.cloned.1.call-update
  48.0 0.5 convolution_convert_fusion.1
  48.4 0.9 copy.12
  49.4 32.9 %all-gather.3.cloned.1.call-done = bf16[512,1280]{1,0:T(8,128)(2,1)} async-done(((bf16[128,1280]{1,0:T(8,128)(2,1)}), bf16[512,1280]{1,0:T(8,128)(2,1)}) %all-gather.3.cloned.1.call-update) | async-done | bytes 1310736 | tf_op jit(solution)/shard_map/all_gather | solution.py:84
  82.2 2.5 %constant_dynamic-update-slice_fusion.1 = bf16[1024,1280]{1,0:T(8,128)(2,1)} fusion(bf16[512,1280]{1,0:T(8,128)(2,1)} %all-gather.3.cloned.1.call-done), kind=kLoop, calls=%fused_computation.54 | loop fusion | bytes 2621440
  84.7 30.8 %all-gather.5.cloned.1.call-done = bf16[512,1280]{1,0:T(8,128)(2,1)} async-done(((bf16[128,1280]{1,0:T(8,128)(2,1)}), bf16[512,1280]{1,0:T(8,128)(2,1)}) %all-gather.5.cloned.1.call-update) | async-done | bytes 1310736 | tf_op jit(solution)/shard_map/all_gather | solution.py:85
  115.5 2.5 %constant_dynamic-update-slice_fusion = bf16[1024,1280]{1,0:T(8,128)(2,1)} fusion(bf16[1024,1280]{1,0:T(8,128)(2,1)} %constant_dynamic-update-slice_fusion.1, bf16[512,1280]{1,0:T(8,128)(2,1)} %all-gather.5.cloned.1.call-done), kind=kLoop, calls=%fused_computation.53 | loop fusion | bytes 2621440 | tf_op jit(solution)/shard_map/concatenate | solution.py:40
  118.0 3.5 %fusion.41 = (bf16[1024,640]{1,0:T(8,128)(2,1)}, bf16[1024,640]{1,0:T(8,128)(2,1)}) fusion(bf16[1024,1280]{1,0:T(8,128)(2,1)} %constant_dynamic-update-slice_fusion), kind=kLoop, calls=%fused_computation.63 | loop fusion | bytes 5242880 | tf_op jit(solution)/shard_map/slice | solution.py:41
  121.5 1.6 copy.13
  123.1 2.5 %copy.14 = bf16[1024,640]{0,1:T(8,128)(2,1)} copy(bf16[1024,640]{1,0:T(8,128)(2,1)} %get-tuple-element.8) | data formatting | bytes 2621440 | tf_op jit(solution)/shard_map/slice | solution.py:42
  125.5 2.6 %multiply_reduce_fusion = (f32[10,256]{1,0:T(8,128)S(1)}, f32[10,256,1024]{2,1,0:T(8,128)S(1)}) fusion(bf16[256,10,64]{0,2,1:T(8,128)(2,1)} %bitcast.74, bf16[1024,10,64]{0,2,1:T(8,128)(2,1)S(1)} %bitcast.69), kind=kOutput, calls=%fused_computation.2 | convolution fusion | flops 340784640 | bytes 12134400 | tf_op jit(solution)/shard_map/qhd,khd->hqk/dot_general | solution.py:43
  128.2 2.1 %fusion = f32[10,256]{1,0:T(8,128)S(1)} fusion(f32[10,256,1024]{2,1,0:T(8,128)S(1)} %get-tuple-element.26, f32[10,256]{1,0:T(8,128)S(1)} %get-tuple-element.20), kind=kLoop, calls=%fused_computation.3 | loop fusion | flops 7861760 | bytes 10506240 | tf_op jit(solution)/shard_map/reduce_sum | solution.py:49
  130.3 2.3 %fusion.19 = bf16[256,10,64]{0,2,1:T(8,128)(2,1)S(1)} fusion(bf16[1024,10,64]{0,2,1:T(8,128)(2,1)S(1)} %bitcast.77, f32[10,256,1024]{2,1,0:T(8,128)S(1)} %get-tuple-element.26, f32[10,256]{1,0:T(8,128)S(1)} %get-tuple-element.20, f32[256,10]{0,1:T(8,128)S(1)} %bitcast.82, f32[256,10]{0,1:T(8,128)S(1)} %get-tuple-element.19), kind=kOutput, calls=%fused_computation.20 | convolution fusion | flops 343900160 | bytes 12154880 | tf_op jit(solution)/shard_map/hqk,khd->qhd/dot_general | solution.py:50
  132.6 0.6 multiply_reduce_fusion.1
  133.4 4.3 %collective-permute-start = (bf16[1,128,640]{2,1,0:T(8,128)(2,1)S(1)}, bf16[1,128,640]{2,1,0:T(8,128)(2,1)S(1)}, u32[]{:S(2)}, u32[]{:S(2)}) collective-permute-start(bf16[1,128,640]{2,1,0:T(8,128)(2,1)S(1)} %get-tuple-element.17), channel_id=1, source_target_pairs={{0,4},{4,8},{8,12},{1,5},{5,9},{9,13},{2,6},{6,10},{10,14},{3,7},{... | collective-permute-start | bytes 491528 | tf_op jit(solution)/shard_map/ppermute | solution.py:24
  137.7 1.9 %collective-permute-start.1 = (bf16[1,128,640]{2,1,0:T(8,128)(2,1)S(1)}, bf16[1,128,640]{2,1,0:T(8,128)(2,1)S(1)}, u32[]{:S(2)}, u32[]{:S(2)}) collective-permute-start(bf16[1,128,640]{2,1,0:T(8,128)(2,1)S(1)} %get-tuple-element.18), channel_id=1, source_target_pairs={{4,0},{8,4},{12,8},{5,1},{9,5},{13,9},{6,2},{10,6},{14,10},{7,3},{... | collective-permute-start | bytes 491528 | tf_op jit(solution)/shard_map/ppermute | solution.py:25
  139.6 0.5 fusion.29
  140.1 4.2 %collective-permute-done.1 = bf16[1,128,640]{2,1,0:T(8,128)(2,1)S(1)} collective-permute-done((bf16[1,128,640]{2,1,0:T(8,128)(2,1)S(1)}, bf16[1,128,640]{2,1,0:T(8,128)(2,1)S(1)}, u32[]{:S(2)}, u32[]{:S(2)}) %collective-permute-start.1) | collective-permute-done | bytes 163872 | tf_op jit(solution)/shard_map/ppermute | solution.py:25
  144.4 0.5 fusion.27
  144.9 0.5 multiply_convert_fusion
  145.4 2.1 %collective-permute-start.2 = (bf16[1,128,640]{2,1,0:T(8,128)(2,1)S(1)}, bf16[1,128,640]{2,1,0:T(8,128)(2,1)S(1)}, u32[]{:S(2)}, u32[]{:S(2)}) collective-permute-start(bf16[1,128,640]{2,1,0:T(8,128)(2,1)S(1)} %get-tuple-element.13), channel_id=1, source_target_pairs={{0,4},{4,8},{8,12},{1,5},{5,9},{9,13},{2,6},{6,10},{10,14},{3,7},{... | collective-permute-start | bytes 491528 | tf_op jit(solution)/shard_map/ppermute | solution.py:24
  147.5 2.4 %collective-permute-start.3 = (bf16[1,128,640]{2,1,0:T(8,128)(2,1)S(1)}, bf16[1,128,640]{2,1,0:T(8,128)(2,1)S(1)}, u32[]{:S(2)}, u32[]{:S(2)}) collective-permute-start(bf16[1,128,640]{2,1,0:T(8,128)(2,1)S(1)} %get-tuple-element.14), channel_id=1, source_target_pairs={{4,0},{8,4},{12,8},{5,1},{9,5},{13,9},{6,2},{10,6},{14,10},{7,3},{... | collective-permute-start | bytes 491528 | tf_op jit(solution)/shard_map/ppermute | solution.py:25
  149.9 0.5 fusion.24
  150.4 3.7 %collective-permute-done.3 = bf16[1,128,640]{2,1,0:T(8,128)(2,1)S(1)} collective-permute-done((bf16[1,128,640]{2,1,0:T(8,128)(2,1)S(1)}, bf16[1,128,640]{2,1,0:T(8,128)(2,1)S(1)}, u32[]{:S(2)}, u32[]{:S(2)}) %collective-permute-start.3) | collective-permute-done | bytes 163872 | tf_op jit(solution)/shard_map/ppermute | solution.py:25
  154.2 0.5 fusion.22
  154.7 1.2 fusion.15
  (31 shorter events, 0.5 us)
Async XLA Ops:
  6.5 4.3 %copy-start = (bf16[640,1280]{1,0:T(8,128)(2,1)S(1)}, bf16[640,1280]{1,0:T(8,128)(2,1)}, u32[]{:S(2)}) copy-start(bf16[640,1280]{1,0:T(8,128)(2,1)} %param.11) | copy-start | bytes 4915204
  6.5 40.7 %all-reduce.3.cloned.1.call-start = ((), (), s32[]{:S(2)}) async-start(), calls=%async_computation.2 | async-start | bytes 1310720 | tf_op jit(solution)/shard_map/psum | solution.py:14
  10.8 37.2 %copy-start.1 = (bf16[2,128,640]{2,1,0:T(8,128)(2,1)S(1)}, bf16[2,128,640]{2,1,0:T(8,128)(2,1)}, u32[]{:S(2)}) copy-start(bf16[2,128,640]{2,1,0:T(8,128)(2,1)} %param.8) | copy-start | bytes 983044
  10.8 37.2 %copy-start.5 = (bf16[640,640]{1,0:T(8,128)(2,1)S(1)}, bf16[640,640]{1,0:T(8,128)(2,1)}, u32[]{:S(2)}) copy-start(bf16[640,640]{1,0:T(8,128)(2,1)} %param.10) | copy-start | bytes 2457604
  12.5 69.8 %all-gather.3.cloned.1.call-start = ((), (), s32[]{:S(2)}) async-start(), calls=%async_computation | async-start | bytes 1638400 | tf_op jit(solution)/shard_map/all_gather | solution.py:84
  47.2 68.3 %all-gather.5.cloned.1.call-start = ((), (), s32[]{:S(2)}) async-start(), calls=%async_computation.1 | async-start | bytes 1638400 | tf_op jit(solution)/shard_map/all_gather | solution.py:85
  128.2 2.1 %copy-start.3 = (bf16[1024,640]{0,1:T(8,128)(2,1)S(1)}, bf16[1024,640]{0,1:T(8,128)(2,1)}, u32[]{:S(2)}) copy-start(bf16[1024,640]{0,1:T(8,128)(2,1)} %copy.14) | copy-start | bytes 3932164
  130.2 2.3 %copy-start.6 = (bf16[640,640]{1,0:T(8,128)(2,1)S(1)}, bf16[640,640]{1,0:T(8,128)(2,1)}, u32[]{:S(2)}) copy-start(bf16[640,640]{1,0:T(8,128)(2,1)} %param.12) | copy-start | bytes 2457604
  130.3 2.9 %copy-start.7 = (f32[640]{0:T(1024)S(1)}, f32[640]{0:T(1024)}, u32[]{:S(2)}) copy-start(f32[640]{0:T(1024)} %param.13) | copy-start | bytes 7684
  132.6 7.1 %copy-start.4 = (bf16[3,640,640]{2,1,0:T(8,128)(2,1)S(1)}, bf16[3,640,640]{2,1,0:T(8,128)(2,1)}, u32[]{:S(2)}) copy-start(bf16[3,640,640]{2,1,0:T(8,128)(2,1)} %param.14) | copy-start | bytes 7372804
  133.4 6.7 %collective-permute-start = (bf16[1,128,640]{2,1,0:T(8,128)(2,1)S(1)}, bf16[1,128,640]{2,1,0:T(8,128)(2,1)S(1)}, u32[]{:S(2)}, u32[]{:S(2)}) collective-permute-start(bf16[1,128,640]{2,1,0:T(8,128)(2,1)S(1)} %get-tuple-element.17), channel_id=1, source_target_pairs={{0,4},{4,8},{8,12},{1,5},{5,9},{9,13},{2,6},{6,10},{10,14},{3,7},{... | collective-permute-start | bytes 491528 | tf_op jit(solution)/shard_map/ppermute | solution.py:24
  137.7 6.6 %collective-permute-start.1 = (bf16[1,128,640]{2,1,0:T(8,128)(2,1)S(1)}, bf16[1,128,640]{2,1,0:T(8,128)(2,1)S(1)}, u32[]{:S(2)}, u32[]{:S(2)}) collective-permute-start(bf16[1,128,640]{2,1,0:T(8,128)(2,1)S(1)} %get-tuple-element.18), channel_id=1, source_target_pairs={{4,0},{8,4},{12,8},{5,1},{9,5},{13,9},{6,2},{10,6},{14,10},{7,3},{... | collective-permute-start | bytes 491528 | tf_op jit(solution)/shard_map/ppermute | solution.py:25
  144.9 5.1 %copy-start.2 = (bf16[3,640,640]{2,1,0:T(8,128)(2,1)S(1)}, bf16[3,640,640]{2,1,0:T(8,128)(2,1)}, u32[]{:S(2)}) copy-start(bf16[3,640,640]{2,1,0:T(8,128)(2,1)} %param.15) | copy-start | bytes 7372804
  145.4 5.0 %collective-permute-start.2 = (bf16[1,128,640]{2,1,0:T(8,128)(2,1)S(1)}, bf16[1,128,640]{2,1,0:T(8,128)(2,1)S(1)}, u32[]{:S(2)}, u32[]{:S(2)}) collective-permute-start(bf16[1,128,640]{2,1,0:T(8,128)(2,1)S(1)} %get-tuple-element.13), channel_id=1, source_target_pairs={{0,4},{4,8},{8,12},{1,5},{5,9},{9,13},{2,6},{6,10},{10,14},{3,7},{... | collective-permute-start | bytes 491528 | tf_op jit(solution)/shard_map/ppermute | solution.py:24
  147.5 6.6 %collective-permute-start.3 = (bf16[1,128,640]{2,1,0:T(8,128)(2,1)S(1)}, bf16[1,128,640]{2,1,0:T(8,128)(2,1)S(1)}, u32[]{:S(2)}, u32[]{:S(2)}) collective-permute-start(bf16[1,128,640]{2,1,0:T(8,128)(2,1)S(1)} %get-tuple-element.14), channel_id=1, source_target_pairs={{4,0},{8,4},{12,8},{5,1},{9,5},{13,9},{6,2},{10,6},{14,10},{7,3},{... | collective-permute-start | bytes 491528 | tf_op jit(solution)/shard_map/ppermute | solution.py:25
Sparse Core Ops, SparseCore 0:
  12.6 34.5 all-reduce.2
  48.8 33.4 all-gather.2
  83.8 31.6 all-gather.4
where the time goes:
time: 163 us; the launch traced here: 162 us
  waiting for transfers between devices  107 us (66%)
  local copies, waits for them, and re-layouts  15.6 us (10%)
  between operations  14.7 us (9%)
  starting transfers between devices  10.8 us (7%)
  matrix products  10.2 us (6%)
  other arithmetic  4.05 us (2%)
    psum x1, waiting for transfers between devices, from_root(): return lax.psum(kept, axis)  34.7 us
    all_gather x1, waiting for transfers between devices, shards(): lax.all_gather(spread_parts[0], 'row', axis=0, tiled=True)  32.9 us
    all_gather x1, waiting for transfers between devices, shards(): lax.all_gather(spread_parts[1], 'row', axis=0, tiled=True)  30.8 us
    ppermute x2, waiting for transfers between devices, extended(): after = lax.ppermute(first, axis, down)  7.96 us
    ppermute x2, starting transfers between devices, extended(): before = lax.ppermute(last, axis, up)  6.37 us
    slice x2, local copies, waits for them, and re-layouts, absorb_keys(): key_heads = joined[:, :channels].reshape(-1, HEADS, HEAD_DIM)  5.06 us
    ppermute x2, starting transfers between devices, extended(): after = lax.ppermute(first, axis, down)  4.33 us
    dot_general x6, matrix products, temporal_mix(): jnp.dot(window, weights[offset], preferred_element_type=jnp.float32)  3.53 us
  transfers between devices with their start and end apart: 7, of which 5 were waited for; matrix products, arithmetic and copies ran while one was open for 3% of the time, Pallas kernels for 0%

commit v1 on v0

v1 whole, which is shorter than its diff:
```python
import functools

import jax
import jax.numpy as jnp
from jax import lax
from jax.experimental import pallas as pl
from jax.experimental.pallas import tpu as pltpu
from jax.sharding import PartitionSpec as P

HEADS = 10
HEAD_DIM = 64
PAIR = 2 * HEAD_DIM
MESH = pl.DeviceIdType.MESH
F32 = jnp.float32
BF16 = jnp.bfloat16


def dot(a, b):
    return jnp.dot(a, b, preferred_element_type=F32)


def kernel(
    F, R,
    frames_ref, key_ref, gain_ref, wq_hbm, wkv_hbm, wo_hbm, w1_hbm, w2_hbm,
    out_ref,
    wq, wkv, wo, w1, w2, kbuf, cand, corebuf, xsrc, xdst,
    q_ref, kv_ref, m_ref, l_ref, acc_ref, att_ref, res_ref, nbuf, hbuf, conv_ref,
    wsem, asend, bsend, brecv, zsend, zrecv, csend, crecv, hsend, hrecv,
):
    T, _, H, C = frames_ref.shape
    N = 2 * H
    M = T * N
    me = lax.axis_index("frame")
    z = lax.axis_index("row")
    c = me % 2
    mate = me + 1 - 2 * c
    bits = F.bit_length() - 1

    loads = [
        pltpu.make_async_copy(src, dst, wsem.at[i])
        for i, (src, dst) in enumerate(
            [(wq_hbm, wq), (wkv_hbm, wkv), (wo_hbm, wo), (w1_hbm, w1), (w2_hbm, w2)]
        )
    ]
    for load in loads:
        load.start()

    barrier = pltpu.get_barrier_semaphore()
    for step in range(1, F):
        pl.semaphore_signal(barrier, 1, device_id={"frame": (me + step) % F}, device_id_type=MESH)
    for hop in (-2, -1, 1, 2):
        there = (z + hop >= 0) & (z + hop < R)

        @pl.when(there)
        def _():
            pl.semaphore_signal(barrier, 1, device_id={"row": z + hop}, device_id_type=MESH)

    other = key_ref[0] + key_ref[1] - (F * T - 1)
    owner = lax.div(other, T)
    local = lax.rem(other, T)
    chosen = frames_ref[0]
    for t in range(1, T):
        chosen = jnp.where(local == t, frames_ref[t], chosen)
    cand[...] = chosen

    @pl.when(me == F - 1)
    def _():
        kbuf[0, z, 1] = frames_ref[T - 1, 1]

    peers = F - 1
    for hop in (-2, -1, 1, 2):
        peers = peers + jnp.where((z + hop >= 0) & (z + hop < R), 1, 0)
    pl.semaphore_wait(barrier, peers)

    def remote(src, dst, ssem, rsem, **device):
        return pltpu.make_async_remote_copy(
            src_ref=src, dst_ref=dst, send_sem=ssem, recv_sem=rsem,
            device_id=device, device_id_type=MESH,
        )

    def last_copy(d):
        return remote(
            frames_ref.at[T - 1, d % 2], kbuf.at[0, z, d % 2],
            asend.at[d], zrecv.at[0, z], frame=d,
        )

    @pl.when(me == F - 1)
    def _():
        for d in range(F - 1):
            last_copy(d).start()

    core_swap = remote(cand.at[1 - c], corebuf, bsend.at[0], brecv.at[0], frame=mate)
    core_swap.start()

    def forward(key, way, d):
        o = z - way * d
        made = []
        for hop in (1, 2):
            dest = z + way * hop
            there = (o >= 0) & (o < R) & (dest >= 0) & (dest < R)
            copy = remote(
                kbuf.at[key, o, c], kbuf.at[key, o, c],
                zsend.at[key, (1 - way) // 2, d // 2, hop - 1], zrecv.at[key, o], row=dest,
            )
            made.append((there, copy))
        return made

    def core_copy(key, o):
        return remote(
            kbuf.at[key, o, c], kbuf.at[key, o, c], csend.at[key, o], crecv.at[key, o], frame=mate
        )

    def start_forward(key, way, d):
        for there, copy in forward(key, way, d):

            @pl.when(there)
            def _():
                copy.start()

    def launch_own(key):
        for way in (1, -1):
            start_forward(key, way, 0)
        core_copy(key, z).start()

    def service(key):
        for d in range(1, R):
            for way in (1, -1):
                o = z - way * d

                @pl.when((o >= 0) & (o < R))
                def _():
                    core_copy_z = remote(
                        kbuf.at[key, o, c], kbuf.at[key, o, c],
                        csend.at[key, o], zrecv.at[key, o], frame=mate,
                    )
                    core_copy_z.wait_recv()
                    if d % 2 == 0:
                        start_forward(key, way, d)
                    core_copy(key, o).start()

    loads[0].wait()
    q = dot(frames_ref[...].reshape(M, C), wq[...]).astype(BF16)
    q_ref[...] = q * BF16(HEAD_DIM ** -0.5)

    core_swap.wait_recv()
    current = jnp.where(lax.rem(owner, 2) == c, cand[c], corebuf[...])

    swaps = []
    for s in range(1, bits):
        bit = (me // 2 ** s) % 2
        partner = me + 2 ** s * (1 - 2 * bit)
        xsrc[s - 1] = current
        swap = remote(xsrc.at[s - 1], xdst.at[s - 1], bsend.at[s], brecv.at[s], frame=partner)
        swap.start()
        swaps.append(swap)
        if s == 1:

            @pl.when(me != F - 1)
            def _():
                remote(
                    frames_ref.at[T - 1, 0], kbuf.at[0, z, c],
                    asend.at[0], zrecv.at[0, z], frame=mate,
                ).wait_recv()

            launch_own(0)
        swap.wait_recv()
        current = jnp.where(lax.rem(lax.div(owner, 2 ** s), 2) == bit, current, xdst[s - 1])
    kbuf[1, z, c] = current
    launch_own(1)

    loads[1].wait()
    lane = lax.broadcasted_iota(jnp.int32, (1, PAIR), 1)
    keys = R * N
    ones = jnp.ones((keys, PAIR), BF16)

    def project(key):
        rows = kbuf[key].reshape(keys, C)

        def column(i, _):
            cols = pl.ds(pl.multiple_of(i * 256, 256), 256)
            kv_ref[:, cols] = dot(rows, wkv[:, cols]).astype(BF16)
            return 0

        lax.fori_loop(0, 2 * C // 256, column, 0)

    def attend(key):
        def pair(i, _):
            cols = pl.ds(pl.multiple_of(i * PAIR, PAIR), PAIR)
            vcols = pl.ds(pl.multiple_of(C + i * PAIR, PAIR), PAIR)
            qp = q_ref[:, cols]
            kp = kv_ref[:, cols]
            vp = jnp.concatenate([kv_ref[:, vcols], ones], axis=1)
            parts = []
            for side in range(2):
                mine = (lane < HEAD_DIM) if side == 0 else (lane >= HEAD_DIM)
                qh = jnp.where(mine, qp, BF16(0))
                scores = lax.dot_general(
                    qh, kp, (((1,), (1,)), ((), ())), preferred_element_type=F32
                )
                top = jnp.max(scores, axis=-1, keepdims=True)
                weights = jnp.exp(scores - top).astype(BF16)
                mixed = dot(weights, vp)
                parts.append((jnp.broadcast_to(top, (M, PAIR)), mixed[:, PAIR:], mixed[:, :PAIR]))
            top, low, acc = [jnp.where(lane < HEAD_DIM, a, b) for a, b in zip(*parts)]
            if key == 0:
                m_ref[:, cols] = top
                l_ref[:, cols] = low
                acc_ref[:, cols] = acc
            else:
                before = m_ref[:, cols]
                raised = jnp.maximum(before, top)
                old = jnp.exp(before - raised)
                new = jnp.exp(top - raised)
                total = acc_ref[:, cols] * old + acc * new
                att_ref[:, cols] = (total / (l_ref[:, cols] * old + low * new)).astype(BF16)
            return 0

        lax.fori_loop(0, HEADS // 2, pair, 0)

    for key in range(2):
        service(key)
        for o in range(R):
            core_copy(key, o).wait_recv()
        project(key)
        attend(key)

    loads[2].wait()
    res = frames_ref[...].reshape(M, C).astype(F32) + dot(att_ref[...], wo[...])
    res_ref[...] = res
    mean_square = jnp.mean(res * res, axis=-1, keepdims=True)
    normed = (res * lax.rsqrt(mean_square + 1e-06) * gain_ref[...]).astype(BF16)
    nbuf[N : N + M] = normed

    def halo(buf, stage):
        up = remote(
            buf.at[pl.ds(M, N)], buf.at[pl.ds(0, N)],
            hsend.at[stage, 0], hrecv.at[stage, 0], frame=(me + 1) % F,
        )
        down = remote(
            buf.at[pl.ds(N, N)], buf.at[pl.ds(N + M, N)],
            hsend.at[stage, 1], hrecv.at[stage, 1], frame=(me + F - 1) % F,
        )
        return up, down

    def start_halo(buf, stage):
        up, down = halo(buf, stage)

        @pl.when(me < F - 1)
        def _():
            up.start()

        @pl.when(me > 0)
        def _():
            down.start()

        @pl.when(me == 0)
        def _():
            buf[0:N] = jnp.zeros((N, C), BF16)

        @pl.when(me == F - 1)
        def _():
            buf[N + M : N + M + N] = jnp.zeros((N, C), BF16)

    def wait_halo(buf, stage):
        up, down = halo(buf, stage)

        @pl.when(me > 0)
        def _():
            up.wait_recv()

        @pl.when(me < F - 1)
        def _():
            down.wait_recv()

    def mix(buf, w, stage):
        inner = dot(buf[N : N + M], w[1])
        conv_ref[...] = inner
        conv_ref[N:M] += dot(buf[N:M], w[0])
        conv_ref[0 : M - N] += dot(buf[2 * N : N + M], w[2])
        wait_halo(buf, stage)
        conv_ref[0:N] += dot(buf[0:N], w[0])
        conv_ref[M - N : M] += dot(buf[N + M : N + M + N], w[2])
        return conv_ref[...]

    start_halo(nbuf, 0)
    loads[3].wait()
    first = mix(nbuf, w1, 0)
    hbuf[N : N + M] = (first / (1.0 + jnp.exp(-first))).astype(BF16)
    start_halo(hbuf, 1)
    loads[4].wait()
    second = mix(hbuf, w2, 1)
    out_ref[...] = (res_ref[...] + second).astype(BF16).reshape(out_ref.shape)

    @pl.when(me == F - 1)
    def _():
        for d in range(F - 1):
            last_copy(d).wait_send()

    core_swap.wait_send()
    for swap in swaps:
        swap.wait_send()
    for key in range(2):
        for o in range(R):
            core_copy(key, o).wait_send()
        for way in (1, -1):
            for d in range(0, R, 2):
                for there, copy in forward(key, way, d):

                    @pl.when(there)
                    def _():
                        copy.wait_send()

    for stage, buf in enumerate((nbuf, hbuf)):
        up, down = halo(buf, stage)

        @pl.when(me < F - 1)
        def _():
            up.wait_send()

        @pl.when(me > 0)
        def _():
            down.wait_send()


def shards(F, R, frames, key_index, w_query, w_keyval, w_out, norm_gain, w_first, w_second):
    T, N, C = frames.shape
    H, M, keys = N // 2, T * N, R * N
    bits = F.bit_length() - 1
    assert F == 2 ** bits and F >= 4
    vmem = pl.BlockSpec(memory_space=pltpu.VMEM)
    any_space = pl.BlockSpec(memory_space=pl.ANY)
    dma = pltpu.SemaphoreType.DMA
    out = pl.pallas_call(
        functools.partial(kernel, F, R),
        out_shape=jax.ShapeDtypeStruct((T, N, C), BF16),
        in_specs=[vmem, pl.BlockSpec(memory_space=pltpu.SMEM), vmem] + [any_space] * 5,
        out_specs=vmem,
        scratch_shapes=[
            pltpu.VMEM(w_query.shape, BF16),
            pltpu.VMEM(w_keyval.shape, BF16),
            pltpu.VMEM(w_out.shape, BF16),
            pltpu.VMEM(w_first.shape, BF16),
            pltpu.VMEM(w_second.shape, BF16),
            pltpu.VMEM((2, R, 2, H, C), BF16),
            pltpu.VMEM((2, H, C), BF16),
            pltpu.VMEM((H, C), BF16),
            pltpu.VMEM((bits - 1, H, C), BF16),
            pltpu.VMEM((bits - 1, H, C), BF16),
            pltpu.VMEM((M, C), BF16),
            pltpu.VMEM((keys, 2 * C), BF16),
            pltpu.VMEM((M, C), F32),
            pltpu.VMEM((M, C), F32),
            pltpu.VMEM((M, C), F32),
            pltpu.VMEM((M, C), BF16),
            pltpu.VMEM((M, C), F32),
            pltpu.VMEM((M + 2 * N, C), BF16),
            pltpu.VMEM((M + 2 * N, C), BF16),
            pltpu.VMEM((M, C), F32),
            dma((5,)),
            dma((F - 1,)),
            dma((bits,)),
            dma((bits,)),
            dma((2, 2, (R + 1) // 2, 2)),
            dma((2, R)),
            dma((2, R)),
            dma((2, R)),
            dma((2, 2)),
            dma((2, 2)),
        ],
        compiler_params=pltpu.CompilerParams(
            collective_id=0, has_side_effects=True, vmem_limit_bytes=48 * 2 ** 20
        ),
        cost_estimate=pl.CostEstimate(
            flops=5 * 10 ** 9, bytes_accessed=9 * 10 ** 6, transcendentals=M * keys * 2 * HEADS
        ),
    )(
        frames.reshape(T, 2, H, C), key_index, norm_gain.reshape(1, C),
        w_query, w_keyval, w_out, w_first, w_second,
    )
    return out


def solution(mesh):
    return jax.shard_map(
        functools.partial(shards, mesh.shape["frame"], mesh.shape["row"]),
        mesh=mesh,
        in_specs=(P(("clips", "frame"), "row", None), P("clips"), P(), P(), P(), P(), P(), P()),
        out_specs=P(("clips", "frame"), "row", None),
        check_vma=False,
    )
```

time: 163 us -> 48 us (0.29)
  waiting for transfers between devices: 107 us -> 0 us
  Pallas kernels: 0 us -> 40.9 us
  between operations: 14.7 us -> 0.01 us
  starting transfers between devices: 10.8 us -> 0 us
  matrix products: 10.2 us -> 0 us
  local copies, waits for them, and re-layouts: 15.6 us -> 6.76 us
  other arithmetic: 4.05 us -> 0 us
    all_gather x2 -> x0, waiting for transfers between devices: 63.7 us -> none  [the longest x1 32.9 us: shards(): lax.all_gather(spread_parts[0], 'row', axis=0, tiled=True)]
    pallas_call x0 -> x1, Pallas kernels: none -> 40.9 us  [shards(): pl.pallas_call(functools.partial(kernel, F, R), out_shape=jax.ShapeDtypeS...]
    psum x1 -> x0, waiting for transfers between devices: 34.7 us -> none  [from_root(): return lax.psum(kept, axis)]
    ppermute x4 -> x0, starting transfers between devices: 10.7 us -> none  [the longest x2 6.37 us: extended(): before = lax.ppermute(last, axis, up)]
    dot_general x11 -> x0, matrix products: 10.2 us -> none  [the longest x6 3.53 us: temporal_mix(): jnp.dot(window, weights[offset], preferred_element_type=jnp.float32)]
    slice x6 -> x0, local copies, waits for them, and re-layouts: 8.17 us -> none  [the longest x2 5.06 us: absorb_keys(): key_heads = joined[:, :channels].reshape(-1, HEADS, HEAD_DIM)]
    ppermute x4 -> x0, waiting for transfers between devices: 7.97 us -> none  [the longest x2 7.96 us: extended(): after = lax.ppermute(first, axis, down)]
    unnamed x17 -> x11, local copies, waits for them, and re-layouts: 2.52 us -> 6.07 us
  transfers between devices with their start and end apart: 7 -> 0, of which waited for: 5 -> 0; matrix products, arithmetic and copies ran while one was open for 3% -> 0% of each run, Pallas kernels for 0% -> 0%
where the time goes in v1:
time: 48 us; the launch traced here: 47.7 us
  Pallas kernels  40.9 us (85%)
  local copies, waits for them, and re-layouts  6.76 us (14%)
    pallas_call x1, Pallas kernels, shards(): pl.pallas_call(functools.partial(kernel, F, R), out_shape=jax.ShapeDtypeS...  40.9 us
    unnamed x11, local copies, waits for them, and re-layouts  6.07 us

profile of v1, /device:TPU:1, one launch (start us, length us, event | category | flops | bytes accessed | tf_op | source)
XLA Modules:
  0.0 47.7 jit_solution(11663448546215096102)
XLA Ops:
  0.0 0.7 %reshape.7.gain_ref = f32[1,640]{1,0:T(1,128)S(1)} reshape(f32[640]{0:T(1024)} %param.13) | data formatting | bytes 5120 | tf_op jit(solution)/shard_map/reshape | solution.py:377
  0.7 0.0 copy-start
  0.7 1.4 %copy-done = bf16[640,1280]{1,0:T(8,128)(2,1)S(1)} copy-done((bf16[640,1280]{1,0:T(8,128)(2,1)S(1)}, bf16[640,1280]{1,0:T(8,128)(2,1)}, u32[]{:S(2)}) %copy-start) | copy-done | bytes 1638424
  2.1 0.0 copy-start.1
  2.1 1.1 %copy-done.1 = bf16[640,640]{1,0:T(8,128)(2,1)S(1)} copy-done((bf16[640,640]{1,0:T(8,128)(2,1)S(1)}, bf16[640,640]{1,0:T(8,128)(2,1)}, u32[]{:S(2)}) %copy-start.1) | copy-done | bytes 819224
  3.3 0.0 copy-start.2
  3.3 1.1 %copy-done.2 = bf16[640,640]{1,0:T(8,128)(2,1)S(1)} copy-done((bf16[640,640]{1,0:T(8,128)(2,1)S(1)}, bf16[640,640]{1,0:T(8,128)(2,1)}, u32[]{:S(2)}) %copy-start.2) | copy-done | bytes 819224
  4.4 0.0 copy-start.3
  4.4 1.0 %copy-done.3 = bf16[2,128,640]{2,1,0:T(8,128)(2,1)S(1)} copy-done((bf16[2,128,640]{2,1,0:T(8,128)(2,1)S(1)}, bf16[2,128,640]{2,1,0:T(8,128)(2,1)}, u32[]{:S(2)}) %copy-start.3) | copy-done | bytes 327704
  5.4 0.0 copy-start.4
  5.4 0.7 %copy-done.4 = s32[2]{0:T(128)S(1)} copy-done((s32[2]{0:T(128)S(1)}, s32[2]{0:T(128)}, u32[]{:S(2)}) %copy-start.4) | copy-done | bytes 32
  6.0 40.9 %shard_map.82 = bf16[2,128,640]{2,1,0:T(8,128)(2,1)S(1)} custom-call(bf16[2,2,64,640]{3,2,1,0:T(8,128)(2,1)S(1)} %bitcast.1, s32[2]{0:T(128)S(1)} %copy-done.4, f32[1,640]{1,0:T(1,128)S(1)} %reshape.7.gain_ref, bf16[640,640]{1,0:T(8,128)(2,1)S(1)} %copy-done.1, bf16[640,1280]{1,0:T(8,128)(2,1)S(1)} %copy-done, bf16[640,640]{1,0:T(8,128)(2,1)S(1)} %copy-done.2, ...), custom_call_target="tpu_custom_call" | custom-call | flops 5000000000 | bytes 9000000 | tf_op jit(solution)/shard_map/pallas_call | solution.py:333
  47.0 0.7 %copy.10 = bf16[2,128,640]{2,1,0:T(8,128)(2,1)} copy(bf16[2,128,640]{2,1,0:T(8,128)(2,1)S(1)} %shard_map.82) | data formatting | bytes 655360
Async XLA Ops:
  0.7 1.4 %copy-start = (bf16[640,1280]{1,0:T(8,128)(2,1)S(1)}, bf16[640,1280]{1,0:T(8,128)(2,1)}, u32[]{:S(2)}) copy-start(bf16[640,1280]{1,0:T(8,128)(2,1)} %wkv_hbm.1) | copy-start | bytes 4915204
  2.1 1.1 %copy-start.1 = (bf16[640,640]{1,0:T(8,128)(2,1)S(1)}, bf16[640,640]{1,0:T(8,128)(2,1)}, u32[]{:S(2)}) copy-start(bf16[640,640]{1,0:T(8,128)(2,1)} %wq_hbm.1) | copy-start | bytes 2457604
  3.3 1.1 %copy-start.2 = (bf16[640,640]{1,0:T(8,128)(2,1)S(1)}, bf16[640,640]{1,0:T(8,128)(2,1)}, u32[]{:S(2)}) copy-start(bf16[640,640]{1,0:T(8,128)(2,1)} %wo_hbm.1) | copy-start | bytes 2457604
  4.4 1.0 %copy-start.3 = (bf16[2,128,640]{2,1,0:T(8,128)(2,1)S(1)}, bf16[2,128,640]{2,1,0:T(8,128)(2,1)}, u32[]{:S(2)}) copy-start(bf16[2,128,640]{2,1,0:T(8,128)(2,1)} %param.8) | copy-start | bytes 983044
  5.4 0.7 %copy-start.4 = (s32[2]{0:T(128)S(1)}, s32[2]{0:T(128)}, u32[]{:S(2)}) copy-start(s32[2]{0:T(128)} %key_ref.1) | copy-start | bytes 28

commit v2 on v1

v2 whole, which is shorter than its diff:
```python
import functools

import jax
import jax.numpy as jnp
from jax import lax
from jax.experimental import pallas as pl
from jax.experimental.pallas import tpu as pltpu
from jax.sharding import PartitionSpec as P

HEADS = 10
HEAD_DIM = 64
PAIR = 2 * HEAD_DIM
MESH = pl.DeviceIdType.MESH
F32 = jnp.float32
BF16 = jnp.bfloat16


def dot(a, b):
    return jnp.dot(a, b, preferred_element_type=F32)


def kernel(
    F, R,
    frames_ref, key_ref, gain_ref, wq_hbm, wkv_hbm, wo_hbm, w1_hbm, w2_hbm,
    out_ref,
    wq, wkv, wo, w1, w2, kbuf, cand, corebuf, xsrc, xdst,
    q_ref, kv_ref, m_ref, l_ref, acc_ref, att_ref, res_ref, nbuf, hbuf, conv_ref, sum_ref,
    wsem, asend, bsend, brecv, zsend, zrecv, xsend, xrecv, csend, crecv, hsend, hrecv,
):
    T, _, _, Q, C = frames_ref.shape
    N = 4 * Q
    M = T * N
    me = lax.axis_index("frame")
    z = lax.axis_index("row")
    c = me % 2
    x = (me // 2) % 2
    mate = me + 1 - 2 * c
    xmate = me + 2 - 4 * x
    bits = F.bit_length() - 1

    loads = [
        pltpu.make_async_copy(src, dst, wsem.at[i])
        for i, (src, dst) in enumerate(
            [(wq_hbm, wq), (wkv_hbm, wkv), (wo_hbm, wo), (w1_hbm, w1), (w2_hbm, w2)]
        )
    ]

    barrier = pltpu.get_barrier_semaphore()
    for step in range(1, F):
        pl.semaphore_signal(barrier, 1, device_id={"frame": (me + step) % F}, device_id_type=MESH)
    for step in range(1, R):
        pl.semaphore_signal(barrier, 1, device_id={"row": (z + step) % R}, device_id_type=MESH)
    for load in loads:
        load.start()

    other = key_ref[0] + key_ref[1] - (F * T - 1)
    owner = lax.div(other, T)
    local = lax.rem(other, T)
    chosen = frames_ref[0]
    for t in range(1, T):
        chosen = jnp.where(local == t, frames_ref[t], chosen)
    cand[...] = chosen

    @pl.when(me == F - 1)
    def _():
        kbuf[0, z, 1] = frames_ref[T - 1, 1]

    pl.semaphore_wait(barrier, F + R - 2)

    def remote(src, dst, ssem, rsem, **device):
        return pltpu.make_async_remote_copy(
            src_ref=src, dst_ref=dst, send_sem=ssem, recv_sem=rsem,
            device_id=device, device_id_type=MESH,
        )

    def last_copy(d):
        return remote(
            frames_ref.at[T - 1, d % 2], kbuf.at[0, z, d % 2],
            asend.at[d], zrecv.at[0, z], frame=d,
        )

    core_swap = remote(cand.at[1 - c], corebuf, bsend.at[0], brecv.at[0], frame=mate)
    core_swap.start()

    @pl.when(me == F - 1)
    def _():
        for d in range(F - 1):
            last_copy(d).start()

    def row_copy(key, way, d):
        dest = z + way * d
        block = kbuf.at[key, z, c] if d == 1 else kbuf.at[key, z, c, x]
        copy = remote(
            block, block, zsend.at[key, (1 - way) // 2, d - 1], zrecv.at[key, z], row=dest
        )
        return (dest >= 0) & (dest < R), copy

    def half_copy(key, o):
        block = kbuf.at[key, o, c]
        return remote(block, block, csend.at[key, o, 0], crecv.at[key, o, 0], frame=mate)

    def quarter_copy(key, o, which):
        block = kbuf.at[key, o, c, which]
        return remote(block, block, csend.at[key, o, which], crecv.at[key, o, which], frame=mate)

    def cross_copy(key, o):
        block = kbuf.at[key, o, c, x]
        return remote(block, block, xsend.at[key, o], xrecv.at[key, o], frame=xmate)

    def await_block(block, sem):
        remote(block, block, csend.at[0, 0, 0], sem, frame=mate).wait_recv()

    def launch_own(key):
        for d in range(1, R):
            for way in (1, -1):
                there, copy = row_copy(key, way, d)

                @pl.when(there)
                def _():
                    copy.start()

        half_copy(key, z).start()

    def origins(d):
        for way in (1, -1):
            o = z - way * d
            yield o, (o >= 0) & (o < R)

    def take_near(key):
        for o, there in origins(1):

            @pl.when(there)
            def _():
                await_block(kbuf.at[key, o, c], zrecv.at[key, o])
                half_copy(key, o).start()

    def take_far(key):
        for d in range(2, R):
            for o, there in origins(d):

                @pl.when(there)
                def _():
                    await_block(kbuf.at[key, o, c, x], zrecv.at[key, o])
                    cross_copy(key, o).start()
                    quarter_copy(key, o, x).start()

    def take_cross(key):
        for d in range(2, R):
            for o, there in origins(d):

                @pl.when(there)
                def _():
                    await_block(kbuf.at[key, o, c, 1 - x], xrecv.at[key, o])
                    quarter_copy(key, o, 1 - x).start()

    def await_near(key):
        await_block(kbuf.at[key, z, 1 - c], crecv.at[key, z, 0])
        for o, there in origins(1):

            @pl.when(there)
            def _():
                await_block(kbuf.at[key, o, 1 - c], crecv.at[key, o, 0])

    def await_far(key):
        for d in range(2, R):
            for o, there in origins(d):

                @pl.when(there)
                def _():
                    for which in range(2):
                        await_block(kbuf.at[key, o, 1 - c, which], crecv.at[key, o, which])

    loads[0].wait()
    q = dot(frames_ref[...].reshape(M, C), wq[...]).astype(BF16)
    q_ref[...] = q * BF16(HEAD_DIM ** -0.5)

    core_swap.wait_recv()
    current = jnp.where(lax.rem(owner, 2) == c, cand[c], corebuf[...])

    swaps = []
    for s in range(1, bits):
        bit = (me // 2 ** s) % 2
        partner = me + 2 ** s * (1 - 2 * bit)
        xsrc[s - 1] = current
        swap = remote(xsrc.at[s - 1], xdst.at[s - 1], bsend.at[s], brecv.at[s], frame=partner)
        swap.start()
        swaps.append(swap)
        if s == 1:

            @pl.when(me != F - 1)
            def _():
                await_block(kbuf.at[0, z, c], zrecv.at[0, z])

            launch_own(0)
        swap.wait_recv()
        current = jnp.where(lax.rem(lax.div(owner, 2 ** s), 2) == bit, current, xdst[s - 1])
    kbuf[1, z, c] = current
    launch_own(1)

    loads[1].wait()
    lane = lax.broadcasted_iota(jnp.int32, (1, PAIR), 1)
    reach = jnp.minimum(z, R - 1 - z)
    onward = jnp.where(z < R - 1 - z, 1, -1)
    per_chunk = 2
    ones = jnp.ones((per_chunk * N, PAIR), BF16)

    def nearest(j):
        d = jnp.where(j <= 2 * reach, (j + 1) // 2, j - reach)
        sign = jnp.where(j <= 2 * reach, 1 - 2 * (j % 2), onward)
        return z + sign * d

    def project(key, chunk):
        rows = jnp.concatenate(
            [kbuf[key, nearest(chunk * per_chunk + i)].reshape(N, C) for i in range(per_chunk)],
            axis=0,
        )
        kv_ref[...] = dot(rows, wkv[...]).astype(BF16)

    def attend(begin, end, rows, count):
        for i in range(HEADS // 2):
            cols = slice(i * PAIR, (i + 1) * PAIR)
            qp = q_ref[rows, cols]
            kp = kv_ref[:, cols]
            vp = jnp.concatenate([kv_ref[:, C + i * PAIR : C + (i + 1) * PAIR], ones], axis=1)
            parts = []
            for side in range(2):
                mine = (lane < HEAD_DIM) if side == 0 else (lane >= HEAD_DIM)
                qh = jnp.where(mine, qp, BF16(0))
                scores = lax.dot_general(
                    qh, kp, (((1,), (1,)), ((), ())), preferred_element_type=F32
                )
                top = jnp.max(scores, axis=-1, keepdims=True)
                weights = jnp.exp(scores - top).astype(BF16)
                mixed = dot(weights, vp)
                parts.append(
                    (jnp.broadcast_to(top, (count, PAIR)), mixed[:, PAIR:], mixed[:, :PAIR])
                )
            top, low, acc = [jnp.where(lane < HEAD_DIM, a, b) for a, b in zip(*parts)]
            if not begin:
                before = m_ref[rows, cols]
                raised = jnp.maximum(before, top)
                old = jnp.exp(before - raised)
                new = jnp.exp(top - raised)
                acc = acc_ref[rows, cols] * old + acc * new
                low = l_ref[rows, cols] * old + low * new
                top = raised
            if end:
                att_ref[rows, cols] = (acc / low).astype(BF16)
            else:
                m_ref[rows, cols] = top
                l_ref[rows, cols] = low
                acc_ref[rows, cols] = acc

    everything = slice(0, M)
    chunks = R // per_chunk
    take_near(0)
    await_near(0)
    project(0, 0)
    attend(True, False, everything, M)
    take_near(1)
    take_far(0)
    await_near(1)
    project(1, 0)
    attend(False, False, everything, M)
    take_cross(0)
    take_far(1)
    await_far(0)
    for chunk in range(1, chunks):
        project(0, chunk)
        attend(False, False, everything, M)
    take_cross(1)
    await_far(1)
    for chunk in range(1, chunks - 1):
        project(1, chunk)
        attend(False, False, everything, M)
    project(1, chunks - 1)

    def up_copy(f):
        k = f - (T - 2)
        return remote(
            nbuf.at[2 + f], nbuf.at[k], hsend.at[0, f], hrecv.at[0, k], frame=(me + 1) % F
        )

    def down_copy(f):
        return remote(
            nbuf.at[2 + f], nbuf.at[T + 2 + f], hsend.at[1, f], hrecv.at[1, f],
            frame=(me + F - 1) % F,
        )

    loads[2].wait()

    @pl.when(me == 0)
    def _():
        nbuf[0:2] = jnp.zeros((2, N, C), BF16)

    @pl.when(me == F - 1)
    def _():
        nbuf[T + 2 : T + 4] = jnp.zeros((2, N, C), BF16)

    for step in range(T):
        f = c * (T - 1 - step) + (1 - c) * step
        rows = pl.ds(pl.multiple_of(f * N, N), N)
        attend(False, True, rows, N)
        res = frames_ref[f].reshape(N, C).astype(F32) + dot(att_ref[rows, :], wo[...])
        res_ref[f] = res
        mean_square = jnp.mean(res * res, axis=-1, keepdims=True)
        gain = gain_ref[...].reshape(1, C)
        nbuf[2 + f] = (res * lax.rsqrt(mean_square + 1e-06) * gain).astype(BF16)

        @pl.when((me < F - 1) & (f >= T - 2))
        def _():
            up_copy(f).start()

        @pl.when((me > 0) & (f < 2))
        def _():
            down_copy(f).start()

    loads[3].wait()
    own = nbuf[2 : T + 2].reshape(M, C)
    for j in range(3):
        part = dot(own, w1[j]).reshape(T, N, C)
        if j == 0:
            conv_ref[0:2] = jnp.zeros((2, N, C), F32)
            conv_ref[2 : T + 2] = part
        else:
            conv_ref[2 - j : T + 2 - j] += part

    def exists(side):
        return ((side == 0) & (me > 0)) | ((side == 1) & (me < F - 1))

    sides = (1 - c, c)
    for side in sides:
        near = 1 + side * (T + 1)

        @pl.when(exists(side))
        def _():
            remote(
                nbuf.at[2], nbuf.at[near], hsend.at[0, 0], hrecv.at[side, 1 - side], frame=mate
            ).wait_recv()

        halo = nbuf[near]
        conv_ref[1 + side * (T - 1)] += dot(halo, w1[2 * side])
        conv_ref[side * (T + 1)] += dot(halo, w1[1])

    def silu(v):
        return v / (1.0 + jnp.exp(-v))

    hbuf[1 : T + 1] = silu(conv_ref[1 : T + 1]).astype(BF16)
    loads[4].wait()
    sum_ref[...] = res_ref[...] + dot(hbuf[1 : T + 1].reshape(M, C), w2[1]).reshape(T, N, C)
    inner = (T - 1) * N
    sum_ref[1:T] += dot(hbuf[1:T].reshape(inner, C), w2[0]).reshape(T - 1, N, C)
    sum_ref[0 : T - 1] += dot(hbuf[2 : T + 1].reshape(inner, C), w2[2]).reshape(T - 1, N, C)
    for side in sides:
        far = side * (T + 3)

        @pl.when(exists(side))
        def _():
            remote(
                nbuf.at[2], nbuf.at[far], hsend.at[0, 0], hrecv.at[side, side], frame=mate
            ).wait_recv()

        value = conv_ref[side * (T + 1)] + dot(nbuf[far], w1[2 * side])
        keep = jnp.where(exists(side), 1.0, 0.0)
        outer = (silu(value) * keep).astype(BF16)
        edge = side * (T - 1)
        sum_ref[edge] += dot(outer, w2[2 * side])
    out_ref[...] = sum_ref[...].astype(BF16)

    @pl.when(me == F - 1)
    def _():
        for d in range(F - 1):
            last_copy(d).wait_send()

    core_swap.wait_send()
    for swap in swaps:
        swap.wait_send()
    for key in range(2):
        half_copy(key, z).wait_send()
        for d in range(1, R):
            for way in (1, -1):
                reached, copy = row_copy(key, way, d)

                @pl.when(reached)
                def _():
                    copy.wait_send()

            for o, came in origins(d):

                @pl.when(came)
                def _():
                    if d == 1:
                        half_copy(key, o).wait_send()
                    else:
                        cross_copy(key, o).wait_send()
                        for which in range(2):
                            quarter_copy(key, o, which).wait_send()

    for f in range(T):

        @pl.when((me < F - 1) & (f >= T - 2))
        def _():
            up_copy(f).wait_send()

        @pl.when((me > 0) & (f < 2))
        def _():
            down_copy(f).wait_send()


def shards(F, R, frames, key_index, w_query, w_keyval, w_out, norm_gain, w_first, w_second):
    T, N, C = frames.shape
    Q, M = N // 4, T * N
    bits = F.bit_length() - 1
    assert F == 2 ** bits and F >= 4 and T >= 2 and R % 2 == 0 and R >= 4
    vmem = pl.BlockSpec(memory_space=pltpu.VMEM)
    any_space = pl.BlockSpec(memory_space=pl.ANY)
    dma = pltpu.SemaphoreType.DMA
    out = pl.pallas_call(
        functools.partial(kernel, F, R),
        out_shape=jax.ShapeDtypeStruct((T, N, C), BF16),
        in_specs=[vmem, pl.BlockSpec(memory_space=pltpu.SMEM), vmem] + [any_space] * 5,
        out_specs=vmem,
        scratch_shapes=[
            pltpu.VMEM(w_query.shape, BF16),
            pltpu.VMEM(w_keyval.shape, BF16),
            pltpu.VMEM(w_out.shape, BF16),
            pltpu.VMEM(w_first.shape, BF16),
            pltpu.VMEM(w_second.shape, BF16),
            pltpu.VMEM((2, R, 2, 2, Q, C), BF16),
            pltpu.VMEM((2, 2, Q, C), BF16),
            pltpu.VMEM((2, Q, C), BF16),
            pltpu.VMEM((bits - 1, 2, Q, C), BF16),
            pltpu.VMEM((bits - 1, 2, Q, C), BF16),
            pltpu.VMEM((M, C), BF16),
            pltpu.VMEM((2 * N, 2 * C), BF16),
            pltpu.VMEM((M, C), F32),
            pltpu.VMEM((M, C), F32),
            pltpu.VMEM((M, C), F32),
            pltpu.VMEM((M, C), BF16),
            pltpu.VMEM((T, N, C), F32),
            pltpu.VMEM((T + 4, N, C), BF16),
            pltpu.VMEM((T + 1, N, C), BF16),
            pltpu.VMEM((T + 2, N, C), F32),
            pltpu.VMEM((T, N, C), F32),
            dma((5,)),
            dma((F - 1,)),
            dma((bits,)),
            dma((bits,)),
            dma((2, 2, R - 1)),
            dma((2, R)),
            dma((2, R)),
            dma((2, R)),
            dma((2, R, 2)),
            dma((2, R, 2)),
            dma((2, T)),
            dma((2, 2)),
        ],
        compiler_params=pltpu.CompilerParams(
            collective_id=0, has_side_effects=True, vmem_limit_bytes=60 * 2 ** 20
        ),
        cost_estimate=pl.CostEstimate(
            flops=5 * 10 ** 9, bytes_accessed=9 * 10 ** 6,
            transcendentals=M * 2 * R * N * HEADS,
        ),
    )(
        frames.reshape(T, 2, 2, Q, C), key_index, norm_gain,
        w_query, w_keyval, w_out, w_first, w_second,
    )
    return out


def solution(mesh):
    return jax.shard_map(
        functools.partial(shards, mesh.shape["frame"], mesh.shape["row"]),
        mesh=mesh,
        in_specs=(P(("clips", "frame"), "row", None), P("clips"), P(), P(), P(), P(), P(), P()),
        out_specs=P(("clips", "frame"), "row", None),
        check_vma=False,
    )
```

time: 48 us -> 35.6 us (0.74)
  Pallas kernels: 40.9 us -> 33.7 us
  local copies, waits for them, and re-layouts: 6.76 us -> 1.73 us
    pallas_call x1, Pallas kernels: 40.9 us -> 33.7 us  [shards(): pl.pallas_call(functools.partial(kernel, F, R), out_shape=jax.ShapeDtypeS...]
    unnamed x11 -> x1, local copies, waits for them, and re-layouts: 6.07 us -> 1.73 us
    reshape x1 -> x0, local copies, waits for them, and re-layouts: 0.69 us -> none  [shards(): norm_gain.reshape(1, C)]
where the time goes in v2:
time: 35.6 us; the launch traced here: 35.4 us
  Pallas kernels  33.7 us (95%)
  local copies, waits for them, and re-layouts  1.73 us (5%)
    pallas_call x1, Pallas kernels, shards(): pl.pallas_call(functools.partial(kernel, F, R), out_shape=jax.ShapeDtypeS...  33.7 us
    unnamed x1, local copies, waits for them, and re-layouts  1.73 us

profile of v2, /device:TPU:1, one launch (start us, length us, event | category | flops | bytes accessed | tf_op | source)
XLA Modules:
  0.0 35.4 jit_solution(12830386698706547705)
XLA Ops:
  0.0 33.7 %shard_map.82 = bf16[2,128,640]{2,1,0:T(8,128)(2,1)} custom-call(bf16[2,2,2,32,640]{4,3,2,1,0:T(8,128)(2,1)} %bitcast.1, s32[2]{0:T(128)} %key_ref.1, f32[640]{0:T(1024)} %gain_ref.1, bf16[640,640]{1,0:T(8,128)(2,1)} %wq_hbm.1, bf16[640,1280]{1,0:T(8,128)(2,1)} %wkv_hbm.1, bf16[640,640]{1,0:T(8,128)(2,1)} %wo_hbm.1, bf16[3,640,640]{2,1,0:T(8,128)(2,1)} %w1_hbm.1, ...), custom_call_target="tpu_custom_call" | custom-call | flops 5000000000 | bytes 9000000 | tf_op jit(solution)/shard_map/pallas_call | solution.py:418
  33.7 1.7 %copy.10 = bf16[2,128,640]{2,1,0:T(8,128)(2,1)} copy(bf16[2,128,640]{2,1,0:T(8,128)(2,1)} %shard_map.82) | data formatting | bytes 655360

commit v3 on v2

--- a/solution.py
+++ b/solution.py
@@ -24,7 +24,7 @@
     frames_ref, key_ref, gain_ref, wq_hbm, wkv_hbm, wo_hbm, w1_hbm, w2_hbm,
     out_ref,
     wq, wkv, wo, w1, w2, kbuf, cand, corebuf, xsrc, xdst,
-    q_ref, kv_ref, m_ref, l_ref, acc_ref, att_ref, res_ref, nbuf, hbuf, conv_ref, sum_ref,
+    q_ref, kv_ref, m_ref, l_ref, acc_ref, att_ref, res_ref, nbuf, hbuf, conv_ref,
     wsem, asend, bsend, brecv, zsend, zrecv, xsend, xrecv, csend, crecv, hsend, hrecv,
 ):
     T, _, _, Q, C = frames_ref.shape
@@ -87,13 +87,18 @@
         for d in range(F - 1):
             last_copy(d).start()
 
-    def row_copy(key, way, d):
-        dest = z + way * d
-        block = kbuf.at[key, z, c] if d == 1 else kbuf.at[key, z, c, x]
-        copy = remote(
-            block, block, zsend.at[key, (1 - way) // 2, d - 1], zrecv.at[key, z], row=dest
-        )
-        return (dest >= 0) & (dest < R), copy
+    near = z + 1 - 2 * (z % 2)
+    others = [
+        2 * ((z // 2 + step) % (R // 2)) + i for step in range(1, R // 2) for i in range(2)
+    ]
+
+    def near_copy(key):
+        block = kbuf.at[key, z, c]
+        return remote(block, block, zsend.at[key, 0], zrecv.at[key, z], row=near)
+
+    def far_copy(key, i):
+        block = kbuf.at[key, z, c, x]
+        return remote(block, block, zsend.at[key, 1 + i], zrecv.at[key, z], row=others[i])
 
     def half_copy(key, o):
         block = kbuf.at[key, o, c]
@@ -111,64 +116,34 @@
         remote(block, block, csend.at[0, 0, 0], sem, frame=mate).wait_recv()
 
     def launch_own(key):
-        for d in range(1, R):
-            for way in (1, -1):
-                there, copy = row_copy(key, way, d)
-
-                @pl.when(there)
-                def _():
-                    copy.start()
-
+        near_copy(key).start()
+        for i in range(R - 2):
+            far_copy(key, i).start()
         half_copy(key, z).start()
 
-    def origins(d):
-        for way in (1, -1):
-            o = z - way * d
-            yield o, (o >= 0) & (o < R)
-
     def take_near(key):
-        for o, there in origins(1):
-
-            @pl.when(there)
-            def _():
-                await_block(kbuf.at[key, o, c], zrecv.at[key, o])
-                half_copy(key, o).start()
+        await_block(kbuf.at[key, near, c], zrecv.at[key, near])
+        half_copy(key, near).start()
 
     def take_far(key):
-        for d in range(2, R):
-            for o, there in origins(d):
-
-                @pl.when(there)
-                def _():
-                    await_block(kbuf.at[key, o, c, x], zrecv.at[key, o])
-                    cross_copy(key, o).start()
-                    quarter_copy(key, o, x).start()
+        for o in others:
+            await_block(kbuf.at[key, o, c, x], zrecv.at[key, o])
+            cross_copy(key, o).start()
+            quarter_copy(key, o, x).start()
 
     def take_cross(key):
-        for d in range(2, R):
-            for o, there in origins(d):
-
-                @pl.when(there)
-                def _():
-                    await_block(kbuf.at[key, o, c, 1 - x], xrecv.at[key, o])
-                    quarter_copy(key, o, 1 - x).start()
+        for o in others:
+            await_block(kbuf.at[key, o, c, 1 - x], xrecv.at[key, o])
+            quarter_copy(key, o, 1 - x).start()
 
     def await_near(key):
-        await_block(kbuf.at[key, z, 1 - c], crecv.at[key, z, 0])
-        for o, there in origins(1):
-
-            @pl.when(there)
-            def _():
-                await_block(kbuf.at[key, o, 1 - c], crecv.at[key, o, 0])
+        for o in (z, near):
+            await_block(kbuf.at[key, o, 1 - c], crecv.at[key, o, 0])
 
     def await_far(key):
-        for d in range(2, R):
-            for o, there in origins(d):
-
-                @pl.when(there)
-                def _():
-                    for which in range(2):
-                        await_block(kbuf.at[key, o, 1 - c, which], crecv.at[key, o, which])
+        for o in others:
+            for which in range(2):
+                await_block(kbuf.at[key, o, 1 - c, which], crecv.at[key, o, which])
 
     loads[0].wait()
     q = dot(frames_ref[...].reshape(M, C), wq[...]).astype(BF16)
@@ -199,21 +174,11 @@
 
     loads[1].wait()
     lane = lax.broadcasted_iota(jnp.int32, (1, PAIR), 1)
-    reach = jnp.minimum(z, R - 1 - z)
-    onward = jnp.where(z < R - 1 - z, 1, -1)
-    per_chunk = 2
-    ones = jnp.ones((per_chunk * N, PAIR), BF16)
-
-    def nearest(j):
-        d = jnp.where(j <= 2 * reach, (j + 1) // 2, j - reach)
-        sign = jnp.where(j <= 2 * reach, 1 - 2 * (j % 2), onward)
-        return z + sign * d
+    ones = jnp.ones((2 * N, PAIR), BF16)
 
     def project(key, chunk):
-        rows = jnp.concatenate(
-            [kbuf[key, nearest(chunk * per_chunk + i)].reshape(N, C) for i in range(per_chunk)],
-            axis=0,
-        )
+        pair = (z // 2 + chunk) % (R // 2)
+        rows = kbuf[key, pl.ds(2 * pair, 2)].reshape(2 * N, C)
         kv_ref[...] = dot(rows, wkv[...]).astype(BF16)
 
     def attend(begin, end, rows, count):
@@ -252,7 +217,7 @@
                 acc_ref[rows, cols] = acc
 
     everything = slice(0, M)
-    chunks = R // per_chunk
+    chunks = R // 2
     take_near(0)
     await_near(0)
     project(0, 0)
@@ -275,17 +240,23 @@
         attend(False, False, everything, M)
     project(1, chunks - 1)
 
-    def up_copy(f):
-        k = f - (T - 2)
+    def up_copy(f, piece):
+        k, rows = f - (T - 2), pl.ds(piece * N // 2, N // 2)
         return remote(
-            nbuf.at[2 + f], nbuf.at[k], hsend.at[0, f], hrecv.at[0, k], frame=(me + 1) % F
+            nbuf.at[2 + f, rows], nbuf.at[k, rows],
+            hsend.at[0, f, piece], hrecv.at[0, k, piece], frame=(me + 1) % F,
         )
 
-    def down_copy(f):
+    def down_copy(f, piece):
+        rows = pl.ds(piece * N // 2, N // 2)
         return remote(
-            nbuf.at[2 + f], nbuf.at[T + 2 + f], hsend.at[1, f], hrecv.at[1, f],
-            frame=(me + F - 1) % F,
+            nbuf.at[2 + f, rows], nbuf.at[T + 2 + f, rows],
+            hsend.at[1, f, piece], hrecv.at[1, f, piece], frame=(me + F - 1) % F,
         )
+
+    def await_halo(side, slot, k):
+        for piece in range(2):
+            await_block(nbuf.at[slot, pl.ds(piece * N // 2, N // 2)], hrecv.at[side, k, piece])
 
     loads[2].wait()
 
@@ -309,11 +280,13 @@
 
         @pl.when((me < F - 1) & (f >= T - 2))
         def _():
-            up_copy(f).start()
+            for piece in range(2):
+                up_copy(f, piece).start()
 
         @pl.when((me > 0) & (f < 2))
         def _():
-            down_copy(f).start()
+            for piece in range(2):
+                down_copy(f, piece).start()
 
     loads[3].wait()
     own = nbuf[2 : T + 2].reshape(M, C)
@@ -330,15 +303,13 @@
 
     sides = (1 - c, c)
     for side in sides:
-        near = 1 + side * (T + 1)
+        beside = 1 + side * (T + 1)
 
         @pl.when(exists(side))
         def _():
-            remote(
-                nbuf.at[2], nbuf.at[near], hsend.at[0, 0], hrecv.at[side, 1 - side], frame=mate
-            ).wait_recv()
-
-        halo = nbuf[near]
+            await_halo(side, beside, 1 - side)
+
+        halo = nbuf[beside]
         conv_ref[1 + side * (T - 1)] += dot(halo, w1[2 * side])
         conv_ref[side * (T + 1)] += dot(halo, w1[1])
 
@@ -347,25 +318,22 @@
 
     hbuf[1 : T + 1] = silu(conv_ref[1 : T + 1]).astype(BF16)
     loads[4].wait()
-    sum_ref[...] = res_ref[...] + dot(hbuf[1 : T + 1].reshape(M, C), w2[1]).reshape(T, N, C)
+    out_ref[...] = res_ref[...] + dot(hbuf[1 : T + 1].reshape(M, C), w2[1]).reshape(T, N, C)
     inner = (T - 1) * N
-    sum_ref[1:T] += dot(hbuf[1:T].reshape(inner, C), w2[0]).reshape(T - 1, N, C)
-    sum_ref[0 : T - 1] += dot(hbuf[2 : T + 1].reshape(inner, C), w2[2]).reshape(T - 1, N, C)
+    out_ref[1:T] += dot(hbuf[1:T].reshape(inner, C), w2[0]).reshape(T - 1, N, C)
+    out_ref[0 : T - 1] += dot(hbuf[2 : T + 1].reshape(inner, C), w2[2]).reshape(T - 1, N, C)
     for side in sides:
         far = side * (T + 3)
 
         @pl.when(exists(side))
         def _():
-            remote(
-                nbuf.at[2], nbuf.at[far], hsend.at[0, 0], hrecv.at[side, side], frame=mate
-            ).wait_recv()
+            await_halo(side, far, side)
 
         value = conv_ref[side * (T + 1)] + dot(nbuf[far], w1[2 * side])
         keep = jnp.where(exists(side), 1.0, 0.0)
         outer = (silu(value) * keep).astype(BF16)
         edge = side * (T - 1)
-        sum_ref[edge] += dot(outer, w2[2 * side])
-    out_ref[...] = sum_ref[...].astype(BF16)
+        out_ref[edge] += dot(outer, w2[2 * side])
 
     @pl.when(me == F - 1)
     def _():
@@ -376,35 +344,26 @@
     for swap in swaps:
         swap.wait_send()
     for key in range(2):
+        near_copy(key).wait_send()
         half_copy(key, z).wait_send()
-        for d in range(1, R):
-            for way in (1, -1):
-                reached, copy = row_copy(key, way, d)
-
-                @pl.when(reached)
-                def _():
-                    copy.wait_send()
-
-            for o, came in origins(d):
-
-                @pl.when(came)
-                def _():
-                    if d == 1:
-                        half_copy(key, o).wait_send()
-                    else:
-                        cross_copy(key, o).wait_send()
-                        for which in range(2):
-                            quarter_copy(key, o, which).wait_send()
+        half_copy(key, near).wait_send()
+        for i, o in enumerate(others):
+            far_copy(key, i).wait_send()
+            cross_copy(key, o).wait_send()
+            for which in range(2):
+                quarter_copy(key, o, which).wait_send()
 
     for f in range(T):
 
         @pl.when((me < F - 1) & (f >= T - 2))
         def _():
-            up_copy(f).wait_send()
+            for piece in range(2):
+                up_copy(f, piece).wait_send()
 
         @pl.when((me > 0) & (f < 2))
         def _():
-            down_copy(f).wait_send()
+            for piece in range(2):
+                down_copy(f, piece).wait_send()
 
 
 def shards(F, R, frames, key_index, w_query, w_keyval, w_out, norm_gain, w_first, w_second):
@@ -417,7 +376,7 @@
     dma = pltpu.SemaphoreType.DMA
     out = pl.pallas_call(
         functools.partial(kernel, F, R),
-        out_shape=jax.ShapeDtypeStruct((T, N, C), BF16),
+        out_shape=jax.ShapeDtypeStruct((T, N, C), F32),
         in_specs=[vmem, pl.BlockSpec(memory_space=pltpu.SMEM), vmem] + [any_space] * 5,
         out_specs=vmem,
         scratch_shapes=[
@@ -441,19 +400,18 @@
             pltpu.VMEM((T + 4, N, C), BF16),
             pltpu.VMEM((T + 1, N, C), BF16),
             pltpu.VMEM((T + 2, N, C), F32),
-            pltpu.VMEM((T, N, C), F32),
             dma((5,)),
             dma((F - 1,)),
             dma((bits,)),
             dma((bits,)),
-            dma((2, 2, R - 1)),
+            dma((2, R - 1)),
             dma((2, R)),
             dma((2, R)),
             dma((2, R)),
             dma((2, R, 2)),
             dma((2, R, 2)),
-            dma((2, T)),
-            dma((2, 2)),
+            dma((2, T, 2)),
+            dma((2, 2, 2)),
         ],
         compiler_params=pltpu.CompilerParams(
             collective_id=0, has_side_effects=True, vmem_limit_bytes=60 * 2 ** 20
@@ -466,7 +424,7 @@
         frames.reshape(T, 2, 2, Q, C), key_index, norm_gain,
         w_query, w_keyval, w_out, w_first, w_second,
     )
-    return out
+    return out.astype(BF16)
 
 
 def solution(mesh):

time: 35.6 us -> 37.6 us (1.056)
  Pallas kernels: 33.7 us -> 35.6 us
  other arithmetic: 0 us -> 1.85 us
  local copies, waits for them, and re-layouts: 1.73 us -> 0 us
    pallas_call x1, Pallas kernels: 33.7 us -> 35.6 us  [shards(): pl.pallas_call(functools.partial(kernel, F, R), out_shape=jax.ShapeDtypeS...]
    convert_element_type x0 -> x1, other arithmetic: none -> 1.85 us  [shards(): return out.astype(BF16)]
    unnamed x1 -> x0, local copies, waits for them, and re-layouts: 1.73 us -> none
where the time goes in v3:
time: 37.6 us; the launch traced here: 37.5 us
  Pallas kernels  35.6 us (95%)
  other arithmetic  1.85 us (5%)
    pallas_call x1, Pallas kernels, shards(): pl.pallas_call(functools.partial(kernel, F, R), out_shape=jax.ShapeDtypeS...  35.6 us
    convert_element_type x1, other arithmetic, shards(): return out.astype(BF16)  1.85 us

profile of v3, /device:TPU:1, one launch (start us, length us, event | category | flops | bytes accessed | tf_op | source)
XLA Modules:
  0.0 37.5 jit_solution(13522458926364732428)
XLA Ops:
  0.0 35.6 %shard_map.82 = f32[2,128,640]{2,1,0:T(8,128)} custom-call(bf16[2,2,2,32,640]{4,3,2,1,0:T(8,128)(2,1)} %bitcast.1, s32[2]{0:T(128)} %key_ref.1, f32[640]{0:T(1024)} %gain_ref.1, bf16[640,640]{1,0:T(8,128)(2,1)} %wq_hbm.1, bf16[640,1280]{1,0:T(8,128)(2,1)} %wkv_hbm.1, bf16[640,640]{1,0:T(8,128)(2,1)} %wo_hbm.1, bf16[3,640,640]{2,1,0:T(8,128)(2,1)} %w1_hbm.1, ...), custom_call_target="tpu_custom_call" | custom-call | flops 5000000000 | bytes 9000000 | tf_op jit(solution)/shard_map/pallas_call | solution.py:377
  35.6 1.8 %convert_element_type.3 = bf16[2,128,640]{2,1,0:T(8,128)(2,1)} convert(f32[2,128,640]{2,1,0:T(8,128)} %shard_map.82) | non-fusion elementwise | flops 163840 | bytes 983040 | tf_op jit(solution)/shard_map/convert_element_type | solution.py:427

commit v4 on v3

--- a/solution.py
+++ b/solution.py
@@ -23,8 +23,8 @@
     F, R,
     frames_ref, key_ref, gain_ref, wq_hbm, wkv_hbm, wo_hbm, w1_hbm, w2_hbm,
     out_ref,
-    wq, wkv, wo, w1, w2, kbuf, cand, corebuf, xsrc, xdst,
-    q_ref, kv_ref, m_ref, l_ref, acc_ref, att_ref, res_ref, nbuf, hbuf, conv_ref,
+    wq, wkv, wo, w1, w2, kbuf, cand, corebuf, xsrc, xdst, raw,
+    q_ref, kv_ref, m_ref, l_ref, acc_ref, att_ref, res_ref, nbuf, hbuf,
     wsem, asend, bsend, brecv, zsend, zrecv, xsend, xrecv, csend, crecv, hsend, hrecv,
 ):
     T, _, _, Q, C = frames_ref.shape
@@ -37,6 +37,8 @@
     mate = me + 1 - 2 * c
     xmate = me + 2 - 4 * x
     bits = F.bit_length() - 1
+    outer = me + 2 * c - 1
+    has_outer = (outer >= 0) & (outer < F)
 
     loads = [
         pltpu.make_async_copy(src, dst, wsem.at[i])
@@ -65,6 +67,10 @@
     def _():
         kbuf[0, z, 1] = frames_ref[T - 1, 1]
 
+    @pl.when((outer < 0) | (outer >= F))
+    def _():
+        raw[...] = jnp.zeros_like(raw)
+
     pl.semaphore_wait(barrier, F + R - 2)
 
     def remote(src, dst, ssem, rsem, **device):
@@ -79,6 +85,14 @@
             asend.at[d], zrecv.at[0, z], frame=d,
         )
 
+    raw_copy = remote(
+        frames_ref.at[pl.ds(c * (T - 2), 2)], raw, hsend.at[0], hrecv.at[0], frame=outer
+    )
+    inner_copy = remote(
+        nbuf.at[pl.ds(2 + (1 - c) * (T - 2), 2)], nbuf.at[pl.ds(c * (T + 2), 2)],
+        hsend.at[1], hrecv.at[1], frame=mate,
+    )
+
     core_swap = remote(cand.at[1 - c], corebuf, bsend.at[0], brecv.at[0], frame=mate)
     core_swap.start()
 
@@ -147,7 +161,7 @@
 
     loads[0].wait()
     q = dot(frames_ref[...].reshape(M, C), wq[...]).astype(BF16)
-    q_ref[...] = q * BF16(HEAD_DIM ** -0.5)
+    q_ref[0:M] = q * BF16(HEAD_DIM ** -0.5)
 
     core_swap.wait_recv()
     current = jnp.where(lax.rem(owner, 2) == c, cand[c], corebuf[...])
@@ -167,6 +181,11 @@
                 await_block(kbuf.at[0, z, c], zrecv.at[0, z])
 
             launch_own(0)
+
+            @pl.when(has_outer)
+            def _():
+                raw_copy.start()
+
         swap.wait_recv()
         current = jnp.where(lax.rem(lax.div(owner, 2 ** s), 2) == bit, current, xdst[s - 1])
     kbuf[1, z, c] = current
@@ -216,124 +235,75 @@
                 l_ref[rows, cols] = low
                 acc_ref[rows, cols] = acc
 
-    everything = slice(0, M)
+    halves = (slice(0, M), slice(M, M + 2 * N))
+
+    def chunk(key, index, begin=False):
+        project(key, index)
+        for rows in halves:
+            attend(begin, False, rows, rows.stop - rows.start)
+
     chunks = R // 2
     take_near(0)
     await_near(0)
     project(0, 0)
-    attend(True, False, everything, M)
+    attend(True, False, halves[0], M)
+
+    @pl.when(has_outer)
+    def _():
+        raw_copy.wait_recv()
+
+    q = dot(raw[...].reshape(2 * N, C), wq[...]).astype(BF16)
+    q_ref[M : M + 2 * N] = q * BF16(HEAD_DIM ** -0.5)
+    take_far(0)
     take_near(1)
-    take_far(0)
+    attend(True, False, halves[1], 2 * N)
     await_near(1)
-    project(1, 0)
-    attend(False, False, everything, M)
+    chunk(1, 0)
     take_cross(0)
     take_far(1)
     await_far(0)
-    for chunk in range(1, chunks):
-        project(0, chunk)
-        attend(False, False, everything, M)
+    for index in range(1, chunks):
+        chunk(0, index)
     take_cross(1)
     await_far(1)
-    for chunk in range(1, chunks - 1):
-        project(1, chunk)
-        attend(False, False, everything, M)
+    for index in range(1, chunks - 1):
+        chunk(1, index)
     project(1, chunks - 1)
-
-    def up_copy(f, piece):
-        k, rows = f - (T - 2), pl.ds(piece * N // 2, N // 2)
-        return remote(
-            nbuf.at[2 + f, rows], nbuf.at[k, rows],
-            hsend.at[0, f, piece], hrecv.at[0, k, piece], frame=(me + 1) % F,
-        )
-
-    def down_copy(f, piece):
-        rows = pl.ds(piece * N // 2, N // 2)
-        return remote(
-            nbuf.at[2 + f, rows], nbuf.at[T + 2 + f, rows],
-            hsend.at[1, f, piece], hrecv.at[1, f, piece], frame=(me + F - 1) % F,
-        )
-
-    def await_halo(side, slot, k):
-        for piece in range(2):
-            await_block(nbuf.at[slot, pl.ds(piece * N // 2, N // 2)], hrecv.at[side, k, piece])
-
     loads[2].wait()
 
-    @pl.when(me == 0)
-    def _():
-        nbuf[0:2] = jnp.zeros((2, N, C), BF16)
-
-    @pl.when(me == F - 1)
-    def _():
-        nbuf[T + 2 : T + 4] = jnp.zeros((2, N, C), BF16)
-
-    for step in range(T):
-        f = c * (T - 1 - step) + (1 - c) * step
-        rows = pl.ds(pl.multiple_of(f * N, N), N)
-        attend(False, True, rows, N)
-        res = frames_ref[f].reshape(N, C).astype(F32) + dot(att_ref[rows, :], wo[...])
-        res_ref[f] = res
+    def finish(rows, tokens):
+        count = rows.stop - rows.start
+        attend(False, True, rows, count)
+        res = tokens.reshape(count, C).astype(F32) + dot(att_ref[rows, :], wo[...])
         mean_square = jnp.mean(res * res, axis=-1, keepdims=True)
         gain = gain_ref[...].reshape(1, C)
-        nbuf[2 + f] = (res * lax.rsqrt(mean_square + 1e-06) * gain).astype(BF16)
-
-        @pl.when((me < F - 1) & (f >= T - 2))
-        def _():
-            for piece in range(2):
-                up_copy(f, piece).start()
-
-        @pl.when((me > 0) & (f < 2))
-        def _():
-            for piece in range(2):
-                down_copy(f, piece).start()
+        normed = (res * lax.rsqrt(mean_square + 1e-06) * gain).astype(BF16)
+        return res.reshape(count // N, N, C), normed.reshape(count // N, N, C)
+
+    res, normed = finish(halves[0], frames_ref[...])
+    res_ref[...] = res
+    nbuf[2 : T + 2] = normed
+    inner_copy.start()
+    _, normed = finish(halves[1], raw[...])
+    nbuf[pl.ds(c * (T + 2), 2)] = jnp.where(has_outer, normed, jnp.zeros_like(normed))
 
     loads[3].wait()
-    own = nbuf[2 : T + 2].reshape(M, C)
-    for j in range(3):
-        part = dot(own, w1[j]).reshape(T, N, C)
-        if j == 0:
-            conv_ref[0:2] = jnp.zeros((2, N, C), F32)
-            conv_ref[2 : T + 2] = part
-        else:
-            conv_ref[2 - j : T + 2 - j] += part
-
-    def exists(side):
-        return ((side == 0) & (me > 0)) | ((side == 1) & (me < F - 1))
-
-    sides = (1 - c, c)
-    for side in sides:
-        beside = 1 + side * (T + 1)
-
-        @pl.when(exists(side))
-        def _():
-            await_halo(side, beside, 1 - side)
-
-        halo = nbuf[beside]
-        conv_ref[1 + side * (T - 1)] += dot(halo, w1[2 * side])
-        conv_ref[side * (T + 1)] += dot(halo, w1[1])
-
-    def silu(v):
-        return v / (1.0 + jnp.exp(-v))
-
-    hbuf[1 : T + 1] = silu(conv_ref[1 : T + 1]).astype(BF16)
     loads[4].wait()
-    out_ref[...] = res_ref[...] + dot(hbuf[1 : T + 1].reshape(M, C), w2[1]).reshape(T, N, C)
-    inner = (T - 1) * N
-    out_ref[1:T] += dot(hbuf[1:T].reshape(inner, C), w2[0]).reshape(T - 1, N, C)
-    out_ref[0 : T - 1] += dot(hbuf[2 : T + 1].reshape(inner, C), w2[2]).reshape(T - 1, N, C)
-    for side in sides:
-        far = side * (T + 3)
-
-        @pl.when(exists(side))
-        def _():
-            await_halo(side, far, side)
-
-        value = conv_ref[side * (T + 1)] + dot(nbuf[far], w1[2 * side])
-        keep = jnp.where(exists(side), 1.0, 0.0)
-        outer = (silu(value) * keep).astype(BF16)
-        edge = side * (T - 1)
-        out_ref[edge] += dot(outer, w2[2 * side])
+    await_block(nbuf.at[pl.ds((1 - c) * (T + 2), 2)], hrecv.at[1])
+    first = sum(dot(nbuf[j : j + T + 2].reshape(M + 2 * N, C), w1[j]) for j in range(3))
+    hidden = first / (1.0 + jnp.exp(-first))
+    hbuf[...] = hidden.astype(BF16).reshape(T + 2, N, C)
+
+    @pl.when(me == 0)
+    def _():
+        hbuf[0] = jnp.zeros((N, C), BF16)
+
+    @pl.when(me == F - 1)
+    def _():
+        hbuf[T + 1] = jnp.zeros((N, C), BF16)
+
+    second = sum(dot(hbuf[j : j + T].reshape(M, C), w2[j]) for j in range(3))
+    out_ref[...] = (res_ref[...] + second.reshape(T, N, C)).astype(BF16)
 
     @pl.when(me == F - 1)
     def _():
@@ -353,17 +323,11 @@
             for which in range(2):
                 quarter_copy(key, o, which).wait_send()
 
-    for f in range(T):
-
-        @pl.when((me < F - 1) & (f >= T - 2))
-        def _():
-            for piece in range(2):
-                up_copy(f, piece).wait_send()
-
-        @pl.when((me > 0) & (f < 2))
-        def _():
-            for piece in range(2):
-                down_copy(f, piece).wait_send()
+    inner_copy.wait_send()
+
+    @pl.when(has_outer)
+    def _():
+        raw_copy.wait_send()
 
 
 def shards(F, R, frames, key_index, w_query, w_keyval, w_out, norm_gain, w_first, w_second):
@@ -372,12 +336,12 @@
     bits = F.bit_length() - 1
     assert F == 2 ** bits and F >= 4 and T >= 2 and R % 2 == 0 and R >= 4
     vmem = pl.BlockSpec(memory_space=pltpu.VMEM)
-    any_space = pl.BlockSpec(memory_space=pl.ANY)
+    hbm = pl.BlockSpec(memory_space=pltpu.HBM)
     dma = pltpu.SemaphoreType.DMA
     out = pl.pallas_call(
         functools.partial(kernel, F, R),
-        out_shape=jax.ShapeDtypeStruct((T, N, C), F32),
-        in_specs=[vmem, pl.BlockSpec(memory_space=pltpu.SMEM), vmem] + [any_space] * 5,
+        out_shape=jax.ShapeDtypeStruct((T, N, C), BF16),
+        in_specs=[vmem, pl.BlockSpec(memory_space=pltpu.SMEM), vmem] + [hbm] * 5,
         out_specs=vmem,
         scratch_shapes=[
             pltpu.VMEM(w_query.shape, BF16),
@@ -390,16 +354,16 @@
             pltpu.VMEM((2, Q, C), BF16),
             pltpu.VMEM((bits - 1, 2, Q, C), BF16),
             pltpu.VMEM((bits - 1, 2, Q, C), BF16),
-            pltpu.VMEM((M, C), BF16),
+            pltpu.VMEM((2, 2, 2, Q, C), BF16),
+            pltpu.VMEM((M + 2 * N, C), BF16),
             pltpu.VMEM((2 * N, 2 * C), BF16),
-            pltpu.VMEM((M, C), F32),
-            pltpu.VMEM((M, C), F32),
-            pltpu.VMEM((M, C), F32),
-            pltpu.VMEM((M, C), BF16),
+            pltpu.VMEM((M + 2 * N, C), F32),
+            pltpu.VMEM((M + 2 * N, C), F32),
+            pltpu.VMEM((M + 2 * N, C), F32),
+            pltpu.VMEM((M + 2 * N, C), BF16),
             pltpu.VMEM((T, N, C), F32),
             pltpu.VMEM((T + 4, N, C), BF16),
-            pltpu.VMEM((T + 1, N, C), BF16),
-            pltpu.VMEM((T + 2, N, C), F32),
+            pltpu.VMEM((T + 2, N, C), BF16),
             dma((5,)),
             dma((F - 1,)),
             dma((bits,)),
@@ -410,8 +374,8 @@
             dma((2, R)),
             dma((2, R, 2)),
             dma((2, R, 2)),
-            dma((2, T, 2)),
-            dma((2, 2, 2)),
+            dma((2,)),
+            dma((2,)),
         ],
         compiler_params=pltpu.CompilerParams(
             collective_id=0, has_side_effects=True, vmem_limit_bytes=60 * 2 ** 20
@@ -424,7 +388,7 @@
         frames.reshape(T, 2, 2, Q, C), key_index, norm_gain,
         w_query, w_keyval, w_out, w_first, w_second,
     )
-    return out.astype(BF16)
+    return out
 
 
 def solution(mesh):

time: 37.6 us -> 37.6 us (level)
  other arithmetic: 1.85 us -> 0 us
  local copies, waits for them, and re-layouts: 0 us -> 1.73 us
    convert_element_type x1 -> x0, other arithmetic: 1.85 us -> none  [shards(): return out.astype(BF16)]
    unnamed x0 -> x1, local copies, waits for them, and re-layouts: none -> 1.73 us
where the time goes in v4:
time: 37.6 us; the launch traced here: 37.3 us
  Pallas kernels  35.6 us (95%)
  local copies, waits for them, and re-layouts  1.73 us (5%)
    pallas_call x1, Pallas kernels, shards(): pl.pallas_call(functools.partial(kernel, F, R), out_shape=jax.ShapeDtypeS...  35.6 us
    unnamed x1, local copies, waits for them, and re-layouts  1.73 us

profile of v4, /device:TPU:1, one launch (start us, length us, event | category | flops | bytes accessed | tf_op | source)
XLA Modules:
  0.0 37.3 jit_solution(2308206984079183514)
XLA Ops:
  0.0 35.6 %shard_map.82 = bf16[2,128,640]{2,1,0:T(8,128)(2,1)} custom-call(bf16[2,2,2,32,640]{4,3,2,1,0:T(8,128)(2,1)} %bitcast.1, s32[2]{0:T(128)} %key_ref.1, f32[640]{0:T(1024)} %gain_ref.1, bf16[640,640]{1,0:T(8,128)(2,1)} %wq_hbm.1, bf16[640,1280]{1,0:T(8,128)(2,1)} %wkv_hbm.1, bf16[640,640]{1,0:T(8,128)(2,1)} %wo_hbm.1, bf16[3,640,640]{2,1,0:T(8,128)(2,1)} %w1_hbm.1, ...), custom_call_target="tpu_custom_call" | custom-call | flops 5000000000 | bytes 9000000 | tf_op jit(solution)/shard_map/pallas_call | solution.py:341
  35.6 1.7 %copy.10 = bf16[2,128,640]{2,1,0:T(8,128)(2,1)} copy(bf16[2,128,640]{2,1,0:T(8,128)(2,1)} %shard_map.82) | data formatting | bytes 655360

commit v5 on v4

--- a/solution.py
+++ b/solution.py
@@ -24,7 +24,7 @@
     frames_ref, key_ref, gain_ref, wq_hbm, wkv_hbm, wo_hbm, w1_hbm, w2_hbm,
     out_ref,
     wq, wkv, wo, w1, w2, kbuf, cand, corebuf, xsrc, xdst, raw,
-    q_ref, kv_ref, m_ref, l_ref, acc_ref, att_ref, res_ref, nbuf, hbuf,
+    wvt, q_ref, k_ref, v_ref, m_ref, l_ref, acc_ref, att_ref, res_ref, nbuf, hbuf,
     wsem, asend, bsend, brecv, zsend, zrecv, xsend, xrecv, csend, crecv, hsend, hrecv,
 ):
     T, _, _, Q, C = frames_ref.shape
@@ -160,8 +160,11 @@
                 await_block(kbuf.at[key, o, 1 - c, which], crecv.at[key, o, which])
 
     loads[0].wait()
-    q = dot(frames_ref[...].reshape(M, C), wq[...]).astype(BF16)
-    q_ref[0:M] = q * BF16(HEAD_DIM ** -0.5)
+    def query(tokens):
+        q = dot(tokens.reshape(tokens.size // C, C), wq[...]).astype(BF16)
+        return jnp.transpose(q * BF16(HEAD_DIM ** -0.5))
+
+    q_ref[:, 0:M] = query(frames_ref[...])
 
     core_swap.wait_recv()
     current = jnp.where(lax.rem(owner, 2) == c, cand[c], corebuf[...])
@@ -192,71 +195,71 @@
     launch_own(1)
 
     loads[1].wait()
-    lane = lax.broadcasted_iota(jnp.int32, (1, PAIR), 1)
-    ones = jnp.ones((2 * N, PAIR), BF16)
+    wvt[...] = jnp.transpose(wkv[:, C:])
+    ones = jnp.ones((16, 2 * N), BF16)
+    blank = jnp.zeros((HEAD_DIM, M), BF16)
 
     def project(key, chunk):
         pair = (z // 2 + chunk) % (R // 2)
         rows = kbuf[key, pl.ds(2 * pair, 2)].reshape(2 * N, C)
-        kv_ref[...] = dot(rows, wkv[...]).astype(BF16)
-
-    def attend(begin, end, rows, count):
-        for i in range(HEADS // 2):
-            cols = slice(i * PAIR, (i + 1) * PAIR)
-            qp = q_ref[rows, cols]
-            kp = kv_ref[:, cols]
-            vp = jnp.concatenate([kv_ref[:, C + i * PAIR : C + (i + 1) * PAIR], ones], axis=1)
-            parts = []
+        k_ref[...] = dot(rows, wkv[:, :C]).astype(BF16)
+        v = lax.dot_general(
+            wvt[...], rows, (((1,), (1,)), ((), ())), preferred_element_type=F32
+        )
+        v_ref[...] = v.astype(BF16)
+
+    def attend(rows):
+        def two_heads(i, _):
+            pair = pl.ds(pl.multiple_of(i * PAIR, PAIR), PAIR)
+            kp = k_ref[:, pair]
+            qp = q_ref[pair, rows]
+            vp = v_ref[pair]
             for side in range(2):
-                mine = (lane < HEAD_DIM) if side == 0 else (lane >= HEAD_DIM)
-                qh = jnp.where(mine, qp, BF16(0))
-                scores = lax.dot_general(
-                    qh, kp, (((1,), (1,)), ((), ())), preferred_element_type=F32
-                )
-                top = jnp.max(scores, axis=-1, keepdims=True)
+                h = 2 * i + side
+                own = pl.ds(pl.multiple_of(h * HEAD_DIM, HEAD_DIM), HEAD_DIM)
+                half = slice(side * HEAD_DIM, (side + 1) * HEAD_DIM)
+                qh = jnp.concatenate([blank, qp[half]] if side else [qp[half], blank], axis=0)
+                scores = dot(kp, qh)
+                before = m_ref[h, :, rows]
+                top = jnp.maximum(jnp.max(scores, axis=0, keepdims=True), before)
                 weights = jnp.exp(scores - top).astype(BF16)
-                mixed = dot(weights, vp)
-                parts.append(
-                    (jnp.broadcast_to(top, (count, PAIR)), mixed[:, PAIR:], mixed[:, :PAIR])
-                )
-            top, low, acc = [jnp.where(lane < HEAD_DIM, a, b) for a, b in zip(*parts)]
-            if not begin:
-                before = m_ref[rows, cols]
-                raised = jnp.maximum(before, top)
-                old = jnp.exp(before - raised)
-                new = jnp.exp(top - raised)
-                acc = acc_ref[rows, cols] * old + acc * new
-                low = l_ref[rows, cols] * old + low * new
-                top = raised
-            if end:
-                att_ref[rows, cols] = (acc / low).astype(BF16)
-            else:
-                m_ref[rows, cols] = top
-                l_ref[rows, cols] = low
-                acc_ref[rows, cols] = acc
-
-    halves = (slice(0, M), slice(M, M + 2 * N))
-
-    def chunk(key, index, begin=False):
+                mixed = dot(jnp.concatenate([vp[half], ones], axis=0), weights)
+                kept = jnp.exp(before - top)
+                m_ref[h, :, rows] = top
+                l_ref[h, :, rows] = l_ref[h, :, rows] * kept + mixed[HEAD_DIM : HEAD_DIM + 1]
+                acc_ref[own, rows] = acc_ref[own, rows] * kept + mixed[:HEAD_DIM]
+            return 0
+
+        lax.fori_loop(0, HEADS // 2, two_heads, 0)
+
+    m_ref[...] = jnp.full_like(m_ref, -1e30)
+    l_ref[...] = jnp.zeros_like(l_ref)
+    acc_ref[...] = jnp.zeros_like(acc_ref)
+    halves = (slice(0, M), slice(M, 2 * M))
+
+    def chunk(key, index):
         project(key, index)
-        for rows in halves:
-            attend(begin, False, rows, rows.stop - rows.start)
+
+        def block(i, _):
+            attend(pl.ds(pl.multiple_of(i * M, M), M))
+            return 0
+
+        lax.fori_loop(0, 2, block, 0)
 
     chunks = R // 2
     take_near(0)
     await_near(0)
     project(0, 0)
-    attend(True, False, halves[0], M)
+    attend(halves[0])
 
     @pl.when(has_outer)
     def _():
         raw_copy.wait_recv()
 
-    q = dot(raw[...].reshape(2 * N, C), wq[...]).astype(BF16)
-    q_ref[M : M + 2 * N] = q * BF16(HEAD_DIM ** -0.5)
+    q_ref[:, M : M + 2 * N] = query(raw[...])
     take_far(0)
     take_near(1)
-    attend(True, False, halves[1], 2 * N)
+    attend(halves[1])
     await_near(1)
     chunk(1, 0)
     take_cross(0)
@@ -273,8 +276,13 @@
 
     def finish(rows, tokens):
         count = rows.stop - rows.start
-        attend(False, True, rows, count)
-        res = tokens.reshape(count, C).astype(F32) + dot(att_ref[rows, :], wo[...])
+        attend(rows)
+        for h in range(HEADS):
+            own = slice(h * HEAD_DIM, (h + 1) * HEAD_DIM)
+            att_ref[own, rows] = (acc_ref[own, rows] / l_ref[h, :, rows]).astype(BF16)
+        res = tokens.reshape(count, C).astype(F32) + dot(
+            jnp.transpose(att_ref[:, rows]), wo[...]
+        )
         mean_square = jnp.mean(res * res, axis=-1, keepdims=True)
         gain = gain_ref[...].reshape(1, C)
         normed = (res * lax.rsqrt(mean_square + 1e-06) * gain).astype(BF16)
@@ -334,7 +342,7 @@
     T, N, C = frames.shape
     Q, M = N // 4, T * N
     bits = F.bit_length() - 1
-    assert F == 2 ** bits and F >= 4 and T >= 2 and R % 2 == 0 and R >= 4
+    assert F == 2 ** bits and F >= 4 and T == 2 and R % 2 == 0 and R >= 4
     vmem = pl.BlockSpec(memory_space=pltpu.VMEM)
     hbm = pl.BlockSpec(memory_space=pltpu.HBM)
     dma = pltpu.SemaphoreType.DMA
@@ -355,12 +363,14 @@
             pltpu.VMEM((bits - 1, 2, Q, C), BF16),
             pltpu.VMEM((bits - 1, 2, Q, C), BF16),
             pltpu.VMEM((2, 2, 2, Q, C), BF16),
-            pltpu.VMEM((M + 2 * N, C), BF16),
-            pltpu.VMEM((2 * N, 2 * C), BF16),
-            pltpu.VMEM((M + 2 * N, C), F32),
-            pltpu.VMEM((M + 2 * N, C), F32),
-            pltpu.VMEM((M + 2 * N, C), F32),
-            pltpu.VMEM((M + 2 * N, C), BF16),
+            pltpu.VMEM((C, C), BF16),
+            pltpu.VMEM((C, M + 2 * N), BF16),
+            pltpu.VMEM((2 * N, C), BF16),
+            pltpu.VMEM((C, 2 * N), BF16),
+            pltpu.VMEM((HEADS, 1, M + 2 * N), F32),
+            pltpu.VMEM((HEADS, 1, M + 2 * N), F32),
+            pltpu.VMEM((C, M + 2 * N), F32),
+            pltpu.VMEM((C, M + 2 * N), BF16),
             pltpu.VMEM((T, N, C), F32),
             pltpu.VMEM((T + 4, N, C), BF16),
             pltpu.VMEM((T + 2, N, C), BF16),

time: 37.6 us -> 55.5 us (1.48)
  Pallas kernels: 35.6 us -> 53.5 us
    pallas_call x1, Pallas kernels: 35.6 us -> 53.5 us  [shards(): pl.pallas_call(functools.partial(kernel, F, R), out_shape=jax.ShapeDtypeS...]
where the time goes in v5:
time: 55.5 us; the launch traced here: 55.3 us
  Pallas kernels  53.5 us (96%)
  local copies, waits for them, and re-layouts  1.73 us (3%)
    pallas_call x1, Pallas kernels, shards(): pl.pallas_call(functools.partial(kernel, F, R), out_shape=jax.ShapeDtypeS...  53.5 us
    unnamed x1, local copies, waits for them, and re-layouts  1.73 us

profile of v5, /device:TPU:1, one launch (start us, length us, event | category | flops | bytes accessed | tf_op | source)
XLA Modules:
  0.0 55.3 jit_solution(9876499618755037757)
XLA Ops:
  0.0 53.5 %shard_map.82 = bf16[2,128,640]{2,1,0:T(8,128)(2,1)} custom-call(bf16[2,2,2,32,640]{4,3,2,1,0:T(8,128)(2,1)} %bitcast.1, s32[2]{0:T(128)} %key_ref.1, f32[640]{0:T(1024)} %gain_ref.1, bf16[640,640]{1,0:T(8,128)(2,1)} %wq_hbm.1, bf16[640,1280]{1,0:T(8,128)(2,1)} %wkv_hbm.1, bf16[640,640]{1,0:T(8,128)(2,1)} %wo_hbm.1, bf16[3,640,640]{2,1,0:T(8,128)(2,1)} %w1_hbm.1, ...), custom_call_target="tpu_custom_call" | custom-call | flops 5000000000 | bytes 9000000 | tf_op jit(solution)/shard_map/pallas_call | solution.py:349
  53.5 1.7 %copy.10 = bf16[2,128,640]{2,1,0:T(8,128)(2,1)} copy(bf16[2,128,640]{2,1,0:T(8,128)(2,1)} %shard_map.82) | data formatting | bytes 655360

commit v6 on v5

--- a/solution.py
+++ b/solution.py
@@ -208,49 +208,44 @@
         )
         v_ref[...] = v.astype(BF16)
 
-    def attend(rows):
-        def two_heads(i, _):
-            pair = pl.ds(pl.multiple_of(i * PAIR, PAIR), PAIR)
-            kp = k_ref[:, pair]
-            qp = q_ref[pair, rows]
-            vp = v_ref[pair]
-            for side in range(2):
-                h = 2 * i + side
-                own = pl.ds(pl.multiple_of(h * HEAD_DIM, HEAD_DIM), HEAD_DIM)
-                half = slice(side * HEAD_DIM, (side + 1) * HEAD_DIM)
-                qh = jnp.concatenate([blank, qp[half]] if side else [qp[half], blank], axis=0)
-                scores = dot(kp, qh)
+    def attend(begin, end, rows):
+        for h in range(HEADS):
+            own = slice(h * HEAD_DIM, (h + 1) * HEAD_DIM)
+            pair = slice(h // 2 * PAIR, (h // 2 + 1) * PAIR)
+            qh = q_ref[own, rows]
+            zero = blank[:, : qh.shape[1]]
+            qh = jnp.concatenate([zero, qh] if h % 2 else [qh, zero], axis=0)
+            scores = dot(k_ref[:, pair], qh)
+            top = jnp.max(scores, axis=0, keepdims=True)
+            if not begin:
                 before = m_ref[h, :, rows]
-                top = jnp.maximum(jnp.max(scores, axis=0, keepdims=True), before)
-                weights = jnp.exp(scores - top).astype(BF16)
-                mixed = dot(jnp.concatenate([vp[half], ones], axis=0), weights)
+                top = jnp.maximum(top, before)
+            weights = jnp.exp(scores - top).astype(BF16)
+            mixed = dot(jnp.concatenate([v_ref[own], ones], axis=0), weights)
+            acc, low = mixed[:HEAD_DIM], mixed[HEAD_DIM : HEAD_DIM + 1]
+            if not begin:
                 kept = jnp.exp(before - top)
+                acc = acc_ref[own, rows] * kept + acc
+                low = l_ref[h, :, rows] * kept + low
+            if end:
+                att_ref[own, rows] = (acc / low).astype(BF16)
+            else:
                 m_ref[h, :, rows] = top
-                l_ref[h, :, rows] = l_ref[h, :, rows] * kept + mixed[HEAD_DIM : HEAD_DIM + 1]
-                acc_ref[own, rows] = acc_ref[own, rows] * kept + mixed[:HEAD_DIM]
-            return 0
-
-        lax.fori_loop(0, HEADS // 2, two_heads, 0)
-
-    m_ref[...] = jnp.full_like(m_ref, -1e30)
-    l_ref[...] = jnp.zeros_like(l_ref)
-    acc_ref[...] = jnp.zeros_like(acc_ref)
-    halves = (slice(0, M), slice(M, 2 * M))
-
-    def chunk(key, index):
+                l_ref[h, :, rows] = low
+                acc_ref[own, rows] = acc
+
+    halves = (slice(0, M), slice(M, M + 2 * N))
+
+    def chunk(key, index, begin=False):
         project(key, index)
-
-        def block(i, _):
-            attend(pl.ds(pl.multiple_of(i * M, M), M))
-            return 0
-
-        lax.fori_loop(0, 2, block, 0)
+        for rows in halves:
+            attend(begin, False, rows)
 
     chunks = R // 2
     take_near(0)
     await_near(0)
     project(0, 0)
-    attend(halves[0])
+    attend(True, False, halves[0])
 
     @pl.when(has_outer)
     def _():
@@ -259,7 +254,7 @@
     q_ref[:, M : M + 2 * N] = query(raw[...])
     take_far(0)
     take_near(1)
-    attend(halves[1])
+    attend(True, False, halves[1])
     await_near(1)
     chunk(1, 0)
     take_cross(0)
@@ -276,10 +271,7 @@
 
     def finish(rows, tokens):
         count = rows.stop - rows.start
-        attend(rows)
-        for h in range(HEADS):
-            own = slice(h * HEAD_DIM, (h + 1) * HEAD_DIM)
-            att_ref[own, rows] = (acc_ref[own, rows] / l_ref[h, :, rows]).astype(BF16)
+        attend(False, True, rows)
         res = tokens.reshape(count, C).astype(F32) + dot(
             jnp.transpose(att_ref[:, rows]), wo[...]
         )
@@ -342,7 +334,7 @@
     T, N, C = frames.shape
     Q, M = N // 4, T * N
     bits = F.bit_length() - 1
-    assert F == 2 ** bits and F >= 4 and T == 2 and R % 2 == 0 and R >= 4
+    assert F == 2 ** bits and F >= 4 and T >= 2 and R % 2 == 0 and R >= 4
     vmem = pl.BlockSpec(memory_space=pltpu.VMEM)
     hbm = pl.BlockSpec(memory_space=pltpu.HBM)
     dma = pltpu.SemaphoreType.DMA

time: 55.5 us -> 50.3 us (0.906)
  Pallas kernels: 53.5 us -> 48.3 us
    pallas_call x1, Pallas kernels: 53.5 us -> 48.3 us  [shards(): pl.pallas_call(functools.partial(kernel, F, R), out_shape=jax.ShapeDtypeS...]
where the time goes in v6:
time: 50.3 us; the launch traced here: 50.1 us
  Pallas kernels  48.3 us (96%)
  local copies, waits for them, and re-layouts  1.73 us (3%)
    pallas_call x1, Pallas kernels, shards(): pl.pallas_call(functools.partial(kernel, F, R), out_shape=jax.ShapeDtypeS...  48.3 us
    unnamed x1, local copies, waits for them, and re-layouts  1.73 us

profile of v6, /device:TPU:1, one launch (start us, length us, event | category | flops | bytes accessed | tf_op | source)
XLA Modules:
  0.0 50.1 jit_solution(4035622560417468607)
XLA Ops:
  0.0 48.3 %shard_map.82 = bf16[2,128,640]{2,1,0:T(8,128)(2,1)} custom-call(bf16[2,2,2,32,640]{4,3,2,1,0:T(8,128)(2,1)} %bitcast.1, s32[2]{0:T(128)} %key_ref.1, f32[640]{0:T(1024)} %gain_ref.1, bf16[640,640]{1,0:T(8,128)(2,1)} %wq_hbm.1, bf16[640,1280]{1,0:T(8,128)(2,1)} %wkv_hbm.1, bf16[640,640]{1,0:T(8,128)(2,1)} %wo_hbm.1, bf16[3,640,640]{2,1,0:T(8,128)(2,1)} %w1_hbm.1, ...), custom_call_target="tpu_custom_call" | custom-call | flops 5000000000 | bytes 9000000 | tf_op jit(solution)/shard_map/pallas_call | solution.py:341
  48.3 1.7 %copy.10 = bf16[2,128,640]{2,1,0:T(8,128)(2,1)} copy(bf16[2,128,640]{2,1,0:T(8,128)(2,1)} %shard_map.82) | data formatting | bytes 655360

commit v7 on v3

--- a/solution.py
+++ b/solution.py
@@ -24,7 +24,7 @@
     frames_ref, key_ref, gain_ref, wq_hbm, wkv_hbm, wo_hbm, w1_hbm, w2_hbm,
     out_ref,
     wq, wkv, wo, w1, w2, kbuf, cand, corebuf, xsrc, xdst,
-    q_ref, kv_ref, m_ref, l_ref, acc_ref, att_ref, res_ref, nbuf, hbuf, conv_ref,
+    q_ref, kv_ref, m_ref, l_ref, acc_ref, att_ref, res_ref, nbuf, hbuf, conv_ref, sum_ref,
     wsem, asend, bsend, brecv, zsend, zrecv, xsend, xrecv, csend, crecv, hsend, hrecv,
 ):
     T, _, _, Q, C = frames_ref.shape
@@ -187,19 +187,22 @@
             qp = q_ref[rows, cols]
             kp = kv_ref[:, cols]
             vp = jnp.concatenate([kv_ref[:, C + i * PAIR : C + (i + 1) * PAIR], ones], axis=1)
-            parts = []
-            for side in range(2):
-                mine = (lane < HEAD_DIM) if side == 0 else (lane >= HEAD_DIM)
-                qh = jnp.where(mine, qp, BF16(0))
-                scores = lax.dot_general(
-                    qh, kp, (((1,), (1,)), ((), ())), preferred_element_type=F32
-                )
-                top = jnp.max(scores, axis=-1, keepdims=True)
-                weights = jnp.exp(scores - top).astype(BF16)
-                mixed = dot(weights, vp)
-                parts.append(
-                    (jnp.broadcast_to(top, (count, PAIR)), mixed[:, PAIR:], mixed[:, :PAIR])
-                )
+            blank = jnp.zeros_like(qp)
+            qs = jnp.concatenate(
+                [jnp.where(lane < HEAD_DIM, qp, blank), jnp.where(lane < HEAD_DIM, blank, qp)],
+                axis=0,
+            )
+            scores = lax.dot_general(
+                qs, kp, (((1,), (1,)), ((), ())), preferred_element_type=F32
+            )
+            top = jnp.max(scores, axis=-1, keepdims=True)
+            weights = jnp.exp(scores - top).astype(BF16)
+            mixed = dot(weights, vp)
+            tops = jnp.broadcast_to(top, (2 * count, PAIR))
+            parts = [
+                (tops[part], mixed[part, PAIR:], mixed[part, :PAIR])
+                for part in (slice(0, count), slice(count, 2 * count))
+            ]
             top, low, acc = [jnp.where(lane < HEAD_DIM, a, b) for a, b in zip(*parts)]
             if not begin:
                 before = m_ref[rows, cols]
@@ -318,10 +321,10 @@
 
     hbuf[1 : T + 1] = silu(conv_ref[1 : T + 1]).astype(BF16)
     loads[4].wait()
-    out_ref[...] = res_ref[...] + dot(hbuf[1 : T + 1].reshape(M, C), w2[1]).reshape(T, N, C)
+    sum_ref[...] = res_ref[...] + dot(hbuf[1 : T + 1].reshape(M, C), w2[1]).reshape(T, N, C)
     inner = (T - 1) * N
-    out_ref[1:T] += dot(hbuf[1:T].reshape(inner, C), w2[0]).reshape(T - 1, N, C)
-    out_ref[0 : T - 1] += dot(hbuf[2 : T + 1].reshape(inner, C), w2[2]).reshape(T - 1, N, C)
+    sum_ref[1:T] += dot(hbuf[1:T].reshape(inner, C), w2[0]).reshape(T - 1, N, C)
+    sum_ref[0 : T - 1] += dot(hbuf[2 : T + 1].reshape(inner, C), w2[2]).reshape(T - 1, N, C)
     for side in sides:
         far = side * (T + 3)
 
@@ -333,7 +336,8 @@
         keep = jnp.where(exists(side), 1.0, 0.0)
         outer = (silu(value) * keep).astype(BF16)
         edge = side * (T - 1)
-        out_ref[edge] += dot(outer, w2[2 * side])
+        sum_ref[edge] += dot(outer, w2[2 * side])
+    out_ref[...] = sum_ref[...].astype(BF16)
 
     @pl.when(me == F - 1)
     def _():
@@ -376,7 +380,7 @@
     dma = pltpu.SemaphoreType.DMA
     out = pl.pallas_call(
         functools.partial(kernel, F, R),
-        out_shape=jax.ShapeDtypeStruct((T, N, C), F32),
+        out_shape=jax.ShapeDtypeStruct((T, N, C), BF16),
         in_specs=[vmem, pl.BlockSpec(memory_space=pltpu.SMEM), vmem] + [any_space] * 5,
         out_specs=vmem,
         scratch_shapes=[
@@ -400,6 +404,7 @@
             pltpu.VMEM((T + 4, N, C), BF16),
             pltpu.VMEM((T + 1, N, C), BF16),
             pltpu.VMEM((T + 2, N, C), F32),
+            pltpu.VMEM((T, N, C), F32),
             dma((5,)),
             dma((F - 1,)),
             dma((bits,)),
@@ -424,7 +429,7 @@
         frames.reshape(T, 2, 2, Q, C), key_index, norm_gain,
         w_query, w_keyval, w_out, w_first, w_second,
     )
-    return out.astype(BF16)
+    return out
 
 
 def solution(mesh):

time: 37.6 us -> 36.8 us (0.979)
  other arithmetic: 1.85 us -> 0 us
  local copies, waits for them, and re-layouts: 0 us -> 1.73 us
  Pallas kernels: 35.6 us -> 34.9 us
    convert_element_type x1 -> x0, other arithmetic: 1.85 us -> none  [shards(): return out.astype(BF16)]
    unnamed x0 -> x1, local copies, waits for them, and re-layouts: none -> 1.73 us
    pallas_call x1, Pallas kernels: 35.6 us -> 34.9 us  [shards(): pl.pallas_call(functools.partial(kernel, F, R), out_shape=jax.ShapeDtypeS...]
where the time goes in v7:
time: 36.8 us; the launch traced here: 36.7 us
  Pallas kernels  34.9 us (95%)
  local copies, waits for them, and re-layouts  1.73 us (5%)
    pallas_call x1, Pallas kernels, shards(): pl.pallas_call(functools.partial(kernel, F, R), out_shape=jax.ShapeDtypeS...  34.9 us
    unnamed x1, local copies, waits for them, and re-layouts  1.73 us

profile of v7, /device:TPU:1, one launch (start us, length us, event | category | flops | bytes accessed | tf_op | source)
XLA Modules:
  0.0 36.7 jit_solution(7519772044725835390)
XLA Ops:
  0.0 34.9 %shard_map.82 = bf16[2,128,640]{2,1,0:T(8,128)(2,1)} custom-call(bf16[2,2,2,32,640]{4,3,2,1,0:T(8,128)(2,1)} %bitcast.1, s32[2]{0:T(128)} %key_ref.1, f32[640]{0:T(1024)} %gain_ref.1, bf16[640,640]{1,0:T(8,128)(2,1)} %wq_hbm.1, bf16[640,1280]{1,0:T(8,128)(2,1)} %wkv_hbm.1, bf16[640,640]{1,0:T(8,128)(2,1)} %wo_hbm.1, bf16[3,640,640]{2,1,0:T(8,128)(2,1)} %w1_hbm.1, ...), custom_call_target="tpu_custom_call" | custom-call | flops 5000000000 | bytes 9000000 | tf_op jit(solution)/shard_map/pallas_call | solution.py:381
  34.9 1.7 %copy.10 = bf16[2,128,640]{2,1,0:T(8,128)(2,1)} copy(bf16[2,128,640]{2,1,0:T(8,128)(2,1)} %shard_map.82) | data formatting | bytes 655360
